TPU v7x, 256 devices: a whole 4x4x8 slice. The times are simulated.
256 devices in a mesh: pre: 4 (over z_hi), grp: 4 (over y), dec: 16 (over x, z_lo, core).
Axes of the slice: x: 4, y: 4, z: 8 (z_hi: 4, z_lo: 2; z = z_hi * 2 + z_lo), core: 2. Of those that a mesh axis runs over, the one named last changes fastest.
Arguments:
- cache: bfloat16 [64, 16384, 576], P('grp', ('pre', 'dec')), may hold values from -300 to 300
- cache_len: int32 [64], P('grp'), may hold values from 1 to 16384
- new_latent: bfloat16 [32, 16384, 576], P('grp', ('pre', 'dec')), may hold values from -6 to 6
- prompt_len: int32 [32], replicated, may hold values from 1 to 16384
- dest: int32 [32, 2], replicated, may hold values from 0 to 15, as said below
- q_latent: bfloat16 [3, 64, 1536], P(None, 'grp'), may hold values from -6 to 6
- new_kv: bfloat16 [3, 64, 576], P(None, 'grp'), may hold values from -6 to 6
- w_uq: bfloat16 [1536, 24576], P(None, ('pre', 'dec')), may hold values from -0.15625 to 0.15625
- w_uk: bfloat16 [128, 128, 512], P(('pre', 'dec')), may hold values from -0.5 to 0.5
- w_uv: bfloat16 [128, 512, 128], P(('pre', 'dec')), may hold values from -3 to 3
- w_o: bfloat16 [16384, 7168], P(('pre', 'dec')), may hold values from -0.125 to 0.125
Outputs:
- attended: bfloat16 [3, 64, 7168], P(None, 'grp', ('pre', 'dec'))
Inputs may be any that keep to these rules, and one draw needn't show every extreme that they name: dest[r,0] is a decode group and dest[r,1] a slot of it; no two requests name the same slot; requests 2k and 2k+1 go to different groups; of the 8 requests in each block of new_latent held by one index of grp, exactly 2 go to each group.
All inputs are finite; a program needn't handle non-finite values.
Results may differ from a plain program's by a relative error of at most 0.035.
The roundings to bfloat16 on the way count: a program that leaves them out, or rounds other values in their place, can miss the bound.
Values may be sent and summed in bfloat16 or wider, within the bound.
A program may use at most 128 MiB of HBM per device.

v0:
```python
import math

import jax
import jax.numpy as jnp
from jax import lax
from jax.sharding import PartitionSpec as P

ROPE_BASE = 10000.0


def rotate(part, positions):
    half = part.shape[-1] // 2
    freq = ROPE_BASE ** (-jnp.arange(half, dtype=jnp.float32) / half)
    angle = positions.astype(jnp.float32)[:, :, None, None] * freq
    first = part[..., :half]
    second = part[..., half:]
    return jnp.concatenate(
        [
            first * jnp.cos(angle) - second * jnp.sin(angle),
            first * jnp.sin(angle) + second * jnp.cos(angle),
        ],
        -1,
    )


def local(cache, cache_len, new_latent, prompt_len, dest, q_latent, new_kv, w_uq, w_uk, w_uv, w_o):
    rows_n, seq_dev, key_dim = cache.shape
    steps_n = q_latent.shape[0]
    heads_dev, nope_dim, latent_dim = w_uk.shape
    scale = 1.0 / math.sqrt(key_dim - latent_dim + nope_dim)
    group = lax.axis_index("grp")
    shard = lax.axis_index("pre") * lax.axis_size("dec") + lax.axis_index("dec")
    arrived = lax.all_gather(new_latent, "grp", axis=0, tiled=True)
    arr_slot = jnp.where(dest[:, 0] == group, dest[:, 1], -1)
    select = arr_slot[:, None] == jnp.arange(rows_n, dtype=jnp.int32)[None, :]
    hit = jnp.any(select, axis=0)
    incoming = jnp.einsum(
        "kr,ksc->rsc", select.astype(jnp.bfloat16), arrived, preferred_element_type=jnp.float32
    ).astype(jnp.bfloat16)
    merged = jnp.where(hit[:, None, None], incoming, cache)
    lengths = jnp.where(hit, jnp.sum(jnp.where(select, prompt_len[:, None], 0), axis=0), cache_len)
    positions = lengths[None, :] + jnp.arange(steps_n, dtype=jnp.int32)[:, None]
    q_full = jnp.dot(
        q_latent.reshape(steps_n * rows_n, -1), w_uq, preferred_element_type=jnp.float32
    )
    q_full = q_full.astype(jnp.bfloat16).reshape(steps_n, rows_n, heads_dev, -1)
    absorbed = jnp.einsum(
        "trhn,hnl->trhl", q_full[..., :nope_dim], w_uk, preferred_element_type=jnp.float32
    ).astype(jnp.bfloat16)
    roped = rotate(q_full[..., nope_dim:].astype(jnp.float32), positions).astype(jnp.bfloat16)
    query = jnp.concatenate([absorbed, roped], -1)
    all_query = lax.all_gather(query, ("pre", "dec"), axis=2, tiled=True)
    place = shard * seq_dev + jnp.arange(seq_dev, dtype=jnp.int32)
    valid = (place[None, :] < lengths[:, None])[None, :, None, :]
    scores = (
        jnp.einsum("trhk,rsk->trhs", all_query, merged, preferred_element_type=jnp.float32) * scale
    )
    masked = jnp.where(valid, scores, jnp.float32(-1e30))
    local_top = jnp.max(masked, axis=-1)
    probs = jnp.where(valid, jnp.exp(masked - local_top[..., None]), jnp.float32(0.0))
    local_total = jnp.sum(probs, axis=-1)
    local_acc = jnp.einsum(
        "trhs,rsl->trhl",
        probs.astype(jnp.bfloat16),
        merged[..., :latent_dim],
        preferred_element_type=jnp.float32,
    )
    tops, totals, accs = (
        lax.all_to_all(local_top[None], ("pre", "dec"), split_axis=3, concat_axis=0, tiled=True),
        lax.all_to_all(local_total[None], ("pre", "dec"), split_axis=3, concat_axis=0, tiled=True),
        lax.all_to_all(local_acc[None], ("pre", "dec"), split_axis=3, concat_axis=0, tiled=True),
    )
    own_top = jnp.max(tops, axis=0)
    factor = jnp.exp(tops - own_top[None])
    own_total = jnp.sum(totals * factor, axis=0)
    own_acc = jnp.sum(accs * factor[..., None], axis=0)
    new_scores = (
        jnp.einsum("trhk,jrk->trhj", query, new_kv, preferred_element_type=jnp.float32) * scale
    )
    causal = (
        jnp.arange(steps_n, dtype=jnp.int32)[None, :]
        <= jnp.arange(steps_n, dtype=jnp.int32)[:, None]
    )[:, None, None, :]
    new_masked = jnp.where(causal, new_scores, jnp.float32(-1e30))
    final_top = jnp.maximum(own_top, jnp.max(new_masked, axis=-1))
    carry_scale = jnp.exp(own_top - final_top)
    new_probs = jnp.where(causal, jnp.exp(new_masked - final_top[..., None]), jnp.float32(0.0))
    full_total = own_total * carry_scale + jnp.sum(new_probs, axis=-1)
    new_acc = jnp.einsum(
        "trhj,jrl->trhl",
        new_probs.astype(jnp.bfloat16),
        new_kv[..., :latent_dim],
        preferred_element_type=jnp.float32,
    )
    full_acc = own_acc * carry_scale[..., None] + new_acc
    latent_out = (full_acc / full_total[..., None]).astype(jnp.bfloat16)
    head_out = jnp.einsum(
        "trhl,hlv->trhv", latent_out, w_uv, preferred_element_type=jnp.float32
    ).astype(jnp.bfloat16)
    flat = head_out.reshape(steps_n * rows_n, -1)
    partial_out = jnp.dot(flat, w_o, preferred_element_type=jnp.float32).reshape(
        steps_n, rows_n, -1
    )
    attended = lax.psum_scatter(partial_out, ("pre", "dec"), scatter_dimension=2, tiled=True)
    return attended.astype(jnp.bfloat16)


def solution(mesh):
    placed = (
        P("grp", ("pre", "dec"), None),
        P("grp"),
        P("grp", ("pre", "dec"), None),
        P(),
        P(),
        P(None, "grp", None),
        P(None, "grp", None),
        P(None, ("pre", "dec")),
        P(("pre", "dec"), None, None),
        P(("pre", "dec"), None, None),
        P(("pre", "dec"), None),
    )
    return jax.shard_map(
        local, mesh=mesh, in_specs=placed, out_specs=P(None, "grp", ("pre", "dec")), check_vma=False
    )
```

profile of v0, /device:TPU:8, one launch (start us, length us, event | category | flops | bytes accessed | tf_op | source)
XLA Modules:
  0.0 898.2 jit_solution(14774517699748372521)
XLA Ops:
  6.6 0.0 all-gather.3.cloned.1.call-start
  6.6 4.5 copy.91
  11.1 0.0 all-gather.3.cloned.1.call-update
  11.1 0.0 all-gather.5.cloned.1.call-start
  11.2 0.3 convolution_convert_fusion.1
  11.5 0.1 reshape.118
  11.7 0.1 fusion.34
  11.8 0.1 select_reduce_fusion
  12.0 0.2 multiply_cosine_fusion
  12.2 0.1 subtract_convert_fusion
  12.3 0.1 fusion.17
  12.4 0.7 pad_maximum_fusion
  13.2 0.0 all-gather.5.cloned.1.call-update
  13.2 0.1 broadcast_compare_fusion
  13.3 98.3 %all-gather.3.cloned.1.call-done = bf16[32,256,576]{1,0,2:T(8,128)(2,1)} async-done(((bf16[8,256,576]{1,0,2:T(8,128)(2,1)}), bf16[32,256,576]{1,0,2:T(8,128)(2,1)}) %all-gather.3.cloned.1.call-update) | async-done | bytes 9437200 | tf_op jit(solution)/shard_map/all_gather | solution.py:33
  111.6 10.4 %copy_select_fusion = bf16[16,256,576]{1,0,2:T(8,128)(2,1)} fusion(bf16[16,256,576]{1,2,0:T(8,128)(2,1)} %param.11, pred[16]{0:T(512)(128)(4,1)S(1)} %fusion.34, bf16[32,256,576]{1,0,2:T(8,128)(2,1)} %all-gather.3.cloned.1.call-done, s32[32]{0:T(128)S(1)} %fusion.37), kind=kOutput, calls=%fused_computation.9 | convolution fusion | flops 155714048 | bytes 18874512 | tf_op jit(solution)/shard_map/kr,ksc->rsc/dot_general | solution.py:37
  122.0 113.1 %all-gather.5.cloned.1.call-done = bf16[3,16,128,576]{3,1,0,2:T(8,128)(2,1)} async-done(((bf16[3,16,2,576]{3,1,0,2:T(8,128)(2,1)}), bf16[3,16,128,576]{3,1,0,2:T(8,128)(2,1)}) %all-gather.5.cloned.1.call-update) | async-done | bytes 7077904 | tf_op jit(solution)/shard_map/all_gather | solution.py:52
  235.1 10.2 %bitcast_reduce_fusion = (f32[3,16,128]{2,0,1:T(4,128)S(1)}, f32[16,256,3,128]{3,1,2,0:T(8,128)S(1)}) fusion(pred[16,256]{1,0:T(8,128)(4,1)S(1)} %broadcast_compare_fusion, bf16[3,16,128,576]{3,1,0,2:T(8,128)(2,1)} %all-gather.5.cloned.1.call-done, bf16[16,256,576,1]{1,0,2,3:T(8,128)(2,1)} %bitcast.93), kind=kOutput, calls=%fused_computation.4 | convolution fusion | flops 1816651776 | bytes 18116608 | tf_op jit(solution)/shard_map/trhk,rsk->trhs/dot_general | solution.py:56
  245.3 2.6 copy-done.2
  248.0 2.0 fusion.5
  250.0 0.8 copy.111
  250.8 8.4 all-to-all-start.2
  259.2 4.5 slice_bitcast_fusion
  263.7 0.8 copy.101
  264.5 6.2 all-to-all-done.2
  270.7 5.0 all-to-all-start.1
  275.8 9.3 %convolution_bitcast_fusion = f32[1,3,16,128,512]{3,4,1,2,0:T(8,128)} fusion(bf16[16,256,512,1]{1,0,2,3:T(8,128)(2,1)} %slice_bitcast_fusion, f32[16,256,3,128]{3,1,2,0:T(8,128)} %copy-done.2, f32[3,16,128]{2,0,1:T(4,128)S(1)} %get-tuple-element.15, pred[16,256]{1,0:T(8,128)(4,1)S(1)} %broadcast_compare_fusion), kind=kOutput, calls=%fused_computation.12 | convolution fusion | flops 1618477056 | bytes 23097344 | tf_op jit(solution)/shard_map/trhs,rsl->trhl/dot_general | solution.py:62
  285.1 12.7 %copy.99 = f32[1,3,16,128,512]{4,2,1,0,3:T(8,128)} copy(f32[1,3,16,128,512]{3,4,1,2,0:T(8,128)} %convolution_bitcast_fusion) | data formatting | bytes 25165824 | tf_op jit(solution)/shard_map/broadcast_in_dim | solution.py:71
  297.8 10.7 %all-to-all-start = ((f32[1,3,16,128,512]{4,2,1,0,3:T(8,128)}), f32[1,3,16,128,512]{4,2,1,0,3:T(8,128)}, u32[]{:S(2)}, u32[]{:S(2)}) async-start(f32[1,3,16,128,512]{4,2,1,0,3:T(8,128)} %copy.99), calls=%async_computation | async-start | bytes 25165824 | tf_op jit(solution)/shard_map/all_to_all | solution.py:71
  308.5 0.0 reduce-scatter.4.cloned.1.call-start
  308.6 1.0 fusion.23
  309.5 0.1 copy.105
  309.7 0.1 bitcast_reduce_fusion.1
  309.8 0.1 reduce_max.28
  309.9 0.1 fusion.41
  310.0 0.1 copy.109
  310.2 0.2 multiply_reduce_fusion.1
  310.4 0.2 fusion.27
  310.5 269.8 %all-to-all-done = f32[1,3,16,128,512]{4,2,1,0,3:T(8,128)} async-done(((f32[1,3,16,128,512]{4,2,1,0,3:T(8,128)}), f32[1,3,16,128,512]{4,2,1,0,3:T(8,128)}, u32[]{:S(2)}, u32[]{:S(2)}) %all-to-all-start) | async-done | bytes 12582944 | tf_op jit(solution)/shard_map/all_to_all | solution.py:71
  580.3 12.1 %copy.100 = f32[1,3,16,128,512]{4,2,3,1,0:T(8,128)} copy(f32[1,3,16,128,512]{4,2,1,0,3:T(8,128)} %all-to-all-done) | data formatting | bytes 25165824 | tf_op jit(solution)/shard_map/all_to_all | solution.py:71
  592.5 6.3 multiply_reduce_fusion
  598.7 0.3 fusion.18
  599.0 0.8 fusion.8
  599.8 9.4 %copy.130 = f32[3,16,7168]{1,0,2:T(4,128)} copy(f32[3,16,7168]{2,1,0:T(8,128)S(1)} %fusion.8) | data formatting | bytes 2752512
  609.1 14.8 %reshape.127 = f32[7168,48]{1,0:T(8,128)} reshape(f32[7168,3,16]{2,1,0:T(4,128)} %bitcast.91) | data formatting | bytes 2752512
  624.0 266.1 %reduce-scatter.4.cloned.1.call-done = f32[112,48]{1,0:T(8,128)} async-done(((f32[7168,48]{1,0:T(8,128)}), f32[112,48]{1,0:T(8,128)}) %reduce-scatter.4.cloned.1.call-update) | async-done | bytes 21520
  890.0 0.9 reshape.128
  891.0 0.7 copy.131
  (39 shorter events, 0.2 us)
Async XLA Ops:
  6.5 4.7 copy-start
  6.5 4.7 copy-start.6
  6.5 5.2 copy-start.8
  6.5 5.3 copy-start.11
  6.5 5.4 copy-start.9
  6.5 5.7 copy-start.5
  6.6 105.0 %all-gather.3.cloned.1.call-start = ((), (), s32[]{:S(2)}) async-start(), calls=%async_computation.4 | async-start | bytes 11796480 | tf_op jit(solution)/shard_map/all_gather | solution.py:33
  11.1 223.9 %all-gather.5.cloned.1.call-start = ((), (), s32[]{:S(2)}) async-start(), calls=%async_computation.5 | async-start | bytes 7987200 | tf_op jit(solution)/shard_map/all_gather | solution.py:52
  245.3 2.6 copy-start.2
  250.8 19.9 %all-to-all-start.2 = ((f32[1,3,16,128]{2,0,1,3:T(1,128)}), f32[1,3,16,128]{2,0,1,3:T(1,128)S(1)}, u32[]{:S(2)}, u32[]{:S(2)}) async-start(f32[1,3,16,128]{2,0,1,3:T(1,128)} %copy.111), calls=%async_computation.2 | async-start | bytes 393216 | tf_op jit(solution)/shard_map/all_to_all | solution.py:70
  270.7 27.0 %all-to-all-start.1 = ((f32[1,3,16,128]{2,0,1,3:T(1,128)}), f32[1,3,16,128]{2,0,1,3:T(1,128)S(1)}, u32[]{:S(2)}, u32[]{:S(2)}) async-start(f32[1,3,16,128]{2,0,1,3:T(1,128)} %copy.101), calls=%async_computation.1 | async-start | bytes 393216 | tf_op jit(solution)/shard_map/all_to_all | solution.py:69
  297.8 10.8 %copy-start.7 = (bf16[3,16,576]{2,1,0:T(8,128)(2,1)S(1)}, bf16[3,16,576]{2,1,0:T(8,128)(2,1)}, u32[]{:S(2)}) copy-start(bf16[3,16,576]{2,1,0:T(8,128)(2,1)} %param.17) | copy-start | bytes 165892
  297.8 10.8 %copy-start.4 = (bf16[3,16,2,576]{3,1,0,2:T(8,128)(2,1)S(1)}, bf16[3,16,2,576]{3,1,0,2:T(8,128)(2,1)}, u32[]{:S(2)}) copy-start(bf16[3,16,2,576]{3,1,0,2:T(8,128)(2,1)} %pad_maximum_fusion) | copy-start | bytes 331780
  297.8 282.6 %all-to-all-start = ((f32[1,3,16,128,512]{4,2,1,0,3:T(8,128)}), f32[1,3,16,128,512]{4,2,1,0,3:T(8,128)}, u32[]{:S(2)}, u32[]{:S(2)}) async-start(f32[1,3,16,128,512]{4,2,1,0,3:T(8,128)} %copy.99), calls=%async_computation | async-start | bytes 25165824 | tf_op jit(solution)/shard_map/all_to_all | solution.py:71
  308.5 581.5 %reduce-scatter.4.cloned.1.call-start = ((), (), s32[]{:S(2)}) async-start(), calls=%async_computation.6 | async-start | bytes 3727360
  592.5 6.3 copy-start.10
  592.5 6.6 copy-start.3
  609.1 282.5 %copy-start.1 = (bf16[1536,384]{1,0:T(8,128)(2,1)S(1)}, bf16[1536,384]{1,0:T(8,128)(2,1)}, u32[]{:S(2)}) copy-start(bf16[1536,384]{1,0:T(8,128)(2,1)} %param.18) | copy-start | bytes 3538948
Sparse Core Ops, SparseCore 0:
  11.3 100.2 all-gather.2
  113.4 121.6 all-gather.4
  624.1 265.9 reduce-scatter.3
where the time goes:
time: 899 us; the launch traced here: 898 us
  waiting for transfers between devices  754 us (84%)
  local copies, waits for them, and re-layouts  64.3 us (7%)
  matrix products  32.6 us (4%)
  starting transfers between devices  24.3 us (3%)
  between operations  13.4 us (1%)
  other arithmetic  10.1 us (1%)
    all_to_all x1, waiting for transfers between devices, local(): lax.all_to_all(local_acc[None], ('pre', 'dec'), split_axis=3, concat_axis...  270 us
    unnamed x4, waiting for transfers between devices  266 us
    all_gather x1, waiting for transfers between devices, local(): all_query = lax.all_gather(query, ('pre', 'dec'), axis=2, tiled=True)  113 us
    all_gather x1, waiting for transfers between devices, local(): arrived = lax.all_gather(new_latent, 'grp', axis=0, tiled=True)  98.3 us
    unnamed x29, local copies, waits for them, and re-layouts  32.9 us
  transfers between devices with their start and end apart: 6, of which 5 were waited for; matrix products, arithmetic and copies ran while one was open for 5% of the time, Pallas kernels for 0%

commit v1 on v0

v1 whole, which is shorter than its diff:
```python
import functools
import math

import jax
import jax.numpy as jnp
from jax import lax
from jax.experimental import pallas as pl
from jax.experimental.pallas import tpu as pltpu
from jax.sharding import PartitionSpec as P

ROPE_BASE = 10000.0
MESH = pl.DeviceIdType.MESH
NEG = -1e30
BF = jnp.bfloat16
F32 = jnp.float32


def up(value, unit):
    return -(-value // unit) * unit


def dot(a, b, **kw):
    return jnp.dot(a, b, preferred_element_type=F32, **kw)


def dot_t(a, b):
    return lax.dot_general(a, b, (((1,), (1,)), ((), ())), preferred_element_type=F32)


def dot_c(a, b):
    return lax.dot_general(a, b, (((0,), (0,)), ((), ())), preferred_element_type=F32)


def onehot(rows, cols, source):
    i = lax.broadcasted_iota(jnp.int32, (rows, cols), 0)
    j = lax.broadcasted_iota(jnp.int32, (rows, cols), 1)
    return jnp.where(source(i) == j, 1.0, 0.0)


def kernel(
    dims,
    dest_ref, clen_ref, plen_ref, freq_ref, ql_ref, nkv_ref, wuq_ref, wuk_ref, wuv_ref,
    cache_ref, newl_ref, wo_ref,
    out_ref,
    cvm, nvm, wov, idx_v, idx, lens_v, sels, sely, pick,
    ysend, yrecv, kx, ko, qh, qsend, pq, ck, qg1, qg2, acc, rsr, st, rss, stm,
    sb, sst, rb, rst, lat, lo, fl, part, po, pr, xr, zs, zr, yos, yor,
    l_s, y_s, y_r, p_s, p_r, a1_s, a1_r, a2_s, a2_r, c_s, c_r, d_s, d_r,
    e_s, e_r, f_s, f_r, x_s, x_r, z_s, z_r, o_s, o_r,
):
    G, NX, NZ, NZL, T, R, HL, PERG, YP, KD, DL, DN, DR, QL, W, SLOTS = dims
    QC = T * 2 * HL
    CH = R * QC
    RT = R * T
    M = 2 * RT
    HM = up(RT, 16)
    RB = R // 2
    KP = up(KD, 128)
    NEW = G * R
    TS = T * SLOTS
    PT = PERG * T
    scale = 1.0 / math.sqrt(DN + DR)
    seq = cache_ref.shape[2]
    pre, grp, dec = lax.axis_index("pre"), lax.axis_index("grp"), lax.axis_index("dec")
    core = lax.rem(dec, 2)
    z = pre * NZL + lax.rem(dec // 2, NZL)
    x = dec // (2 * NZL)
    shard = pre * (2 * NZL * NX) + dec

    def at(xx, zz, cc, gg):
        return (zz // NZL, gg, xx * (2 * NZL) + lax.rem(zz, NZL) * 2 + cc)

    partner = at(x, z, 1 - core, grp)

    def x_peer(k):
        xx = lax.rem(x + k, NX)
        return xx, at(xx, z, core, grp)

    def z_peer(k):
        zz = lax.rem(z + k, NZ)
        return zz, at(x, zz, core, grp)

    def g_peer(k):
        gg = lax.rem(grp + k, G)
        return gg, at(x, z, core, gg)

    def copy(src, dst, s, r, dev):
        return pltpu.make_async_remote_copy(
            src_ref=src, dst_ref=dst, send_sem=s, recv_sem=r, device_id=dev, device_id_type=MESH
        )

    def rows(ref, start, count):
        return ref.at[pl.ds(pl.multiple_of(start, 16), count)]

    def iota(shape, axis):
        return lax.broadcasted_iota(jnp.int32, shape, axis)

    barrier = pltpu.get_barrier_semaphore()
    peers = [partner]
    peers += [x_peer(k)[1] for k in range(1, NX)]
    peers += [z_peer(k)[1] for k in range(1, NZ)]
    peers += [g_peer(k)[1] for k in range(1, G)]
    for dev in peers:
        pl.semaphore_signal(barrier, inc=1, device_id=dev, device_id_type=MESH)
    load_c = pltpu.make_async_copy(cache_ref, cvm, l_s.at[0])
    load_n = pltpu.make_async_copy(newl_ref, nvm, l_s.at[1])
    load_o = pltpu.make_async_copy(wo_ref, wov, l_s.at[2])
    load_c.start()

    to_row = dest_ref[0:1, :]
    spot_row = dest_ref[1:2, :]
    same = iota((NEW, NEW), 0) == iota((NEW, NEW), 1)
    to_col = jnp.sum(jnp.where(same, to_row, 0), axis=1, keepdims=True)
    spot_col = jnp.sum(jnp.where(same, spot_row, 0), axis=1, keepdims=True)
    here_row = to_row == grp
    hit = jnp.where((spot_row == iota((SLOTS, NEW), 0)) & here_row, 1, 0)
    left_col = 1 - jnp.sum(hit, axis=1, keepdims=True)

    def before(shape):
        slot = lax.rem(iota(shape, 1), SLOTS)
        return jnp.sum(jnp.where(iota(shape, 0) < slot, left_col, 0), axis=0, keepdims=True)

    def left(shape):
        slot = lax.rem(iota(shape, 1), SLOTS)
        return jnp.sum(jnp.where(iota(shape, 0) == slot, left_col, 0), axis=0, keepdims=True)

    before_t, left_t = before((SLOTS, TS)), left((SLOTS, TS))
    before_s, left_s = before((SLOTS, SLOTS)), left((SLOTS, SLOTS))
    is_surv = (before_s == iota((2 * R, SLOTS), 0)) & (left_s > 0) & (iota((2 * R, SLOTS), 0) < R)
    surv_col = jnp.sum(jnp.where(is_surv, iota((2 * R, SLOTS), 1), 0), axis=1, keepdims=True)
    idx_v[...] = jnp.broadcast_to(surv_col, idx_v.shape)
    fetch = pltpu.make_async_copy(idx_v, idx, l_s.at[3])
    fetch.start()
    row_of = iota((2 * R, NEW), 0) - R + grp * R
    is_mine = (iota((2 * R, NEW), 1) == row_of) & (iota((2 * R, NEW), 0) >= R)
    lens_col = jnp.sum(jnp.where(is_surv, clen_ref[...], 0), axis=1, keepdims=True) + jnp.sum(
        jnp.where(is_mine, plen_ref[...], 0), axis=1, keepdims=True
    )
    lens_v[...] = jnp.broadcast_to(lens_col, lens_v.shape)
    k_row, k_col = iota((NEW, NEW), 1), iota((NEW, NEW), 0)
    rank_row = jnp.sum(
        jnp.where((to_col == to_row) & (k_col // R == k_row // R) & (k_col < k_row), 1, 0),
        axis=0,
        keepdims=True,
    )
    i, j = iota((M, TS), 0), iota((M, TS), 1)
    sels[...] = jnp.where(
        (before_t == i // T) & (left_t > 0) & (j // SLOTS == i % T) & (i < RT), 1.0, 0.0
    ).astype(BF)
    i, j = iota((G * YP, NEW), 0), iota((G * YP, NEW), 1)
    u = i % YP
    from_k = jnp.where((j // R == i // YP) & here_row & (rank_row == u // T) & (u < PT), 1.0, 0.0)
    to_slot = jnp.where(spot_col == iota((NEW, TS), 1) % SLOTS, 1.0, 0.0)
    i, j = iota((G * YP, TS), 0), iota((G * YP, TS), 1)
    sely[...] = jnp.where(
        j // SLOTS == i % YP % T, dot(from_k.astype(BF), to_slot.astype(BF)), 0.0
    ).astype(BF)
    i, j = iota((M, NEW), 0), iota((M, NEW), 1)
    own_k = (j == (i - RT) // T + grp * R) & (i >= RT)
    key_col = jnp.sum(jnp.where(own_k, to_row * YP + rank_row * T, 0), axis=1, keepdims=True)
    i, j = iota((M, G * YP), 0), iota((M, G * YP), 1)
    pick[...] = jnp.where((key_col + i % T == j) & (i >= RT), 1.0, 0.0).astype(BF)
    ysend[:, :QL] = dot(sely[...], ql_ref[...]).astype(BF)
    ysend[:, QL : QL + KD] = dot(sely[...], nkv_ref[...]).astype(BF)

    pl.semaphore_wait(barrier, len(peers))
    done = []
    for k in range(1, G):
        gg, dev = g_peer(k)
        c = copy(rows(ysend, gg * YP, YP), rows(yrecv, grp * YP, YP), y_s.at[k], y_r.at[grp], dev)
        c.start()
        done.append(c)
    own = pl.ds(pl.multiple_of(grp * YP, 16), YP)
    yrecv[own, :] = ysend[own, :]

    keys = copy(kx, ko, p_s.at[0], p_r.at[0], partner)
    done.append(keys)

    @pl.when(core == 0)
    def _():
        copy(newl_ref, ko, p_s.at[0], p_r.at[0], partner).start()

    fetch.wait()
    load_c.wait()

    @pl.when(core == 1)
    def _():
        for j in range(R):
            kx[j] = cvm[idx[j, 0]]
        keys.start()
        load_n.start()

    load_o.start()

    half_dr = DR // 2
    lens_row = jnp.sum(
        jnp.where(iota((2 * R, 2 * R), 0) == iota((2 * R, 2 * R), 1), lens_col, 0),
        axis=0,
        keepdims=True,
    )

    def produce(half):
        i = iota((HM, 2 * R), 0)
        found = jnp.where((iota((HM, 2 * R), 1) == half * R + i // T) & (i < RT), lens_row, 0)
        pos = jnp.sum(found, axis=1, keepdims=True) + iota((HM, 1), 0) % T
        angle = pos.astype(F32) * freq_ref[...]
        cos, sin = jnp.cos(angle), jnp.sin(angle)
        sin = jnp.where(iota((HM, DR), 1) < half_dr, -sin, sin)
        if half == 0:
            xin = dot(sels[:HM, :], ql_ref[...]).astype(BF)
        else:
            i = iota((HM, M), 0)
            low = jnp.where((iota((HM, M), 1) == i + RT) & (i < RT), 1.0, 0.0).astype(BF)
            xin = dot(dot(low, pick[...]).astype(BF), yrecv[:, :QL]).astype(BF)
        qf = dot(xin, wuq_ref[...]).astype(BF)
        HD = DN + DR
        for h in range(HL):
            nope = dot(qf, onehot(HL * HD, DN, lambda i: i - h * HD).astype(BF)).astype(BF)
            qh[h, :, :DL] = dot(nope, wuk_ref[h]).astype(BF)
            turned = lambda i: jnp.where(
                (i >= h * HD + DN) & (i < (h + 1) * HD), (i - h * HD - DN + half_dr) % DR, -1
            )
            rot = dot(qf, onehot(HL * HD, DR, lambda i: i - h * HD - DN).astype(BF))
            swp = dot(qf, onehot(HL * HD, DR, turned).astype(BF))
            qh[h, :, DL:] = (rot * cos + swp * sin).astype(BF)
        total = None
        for h in range(HL):
            sel = onehot(
                HL * RT,
                HM,
                lambda i: jnp.where((i >= h * RT) & (i < (h + 1) * RT), i - h * RT, -1),
            ).astype(BF)
            term = dot(sel, qh[h])
            total = term if total is None else total + term
        return total.astype(BF)

    def incoming():
        for k in range(1, G):
            gg, dev = g_peer(k)
            copy(
                rows(ysend, gg * YP, YP), rows(yrecv, gg * YP, YP), y_s.at[k], y_r.at[gg], dev
            ).wait_recv()

    def to_partner(block):
        qsend[...] = block
        c = copy(qsend, pq.at[core], p_s.at[1], p_r.at[1], partner)
        c.start()

    def gather_chunk():
        copy(qsend, pq.at[1 - core], p_s.at[1], p_r.at[1], partner).wait_recv()
        regroup = onehot(
            CH, CH, lambda i: i % (2 * HL) * RT + i // QC * T + i % QC // (2 * HL)
        ).astype(BF)
        ck[...] = (dot(regroup, pq[...].reshape(CH, KD))).astype(BF)

    done.append(copy(qsend, pq.at[core], p_s.at[1], p_r.at[1], partner))

    def spread(cc, n1, i1, peer1, n2, i2, peer2):
        w = n1 * QC
        blk = R * w
        sub = RB * w
        sends = []

        def hops(n, b, d):
            return n // 2 if (b == 0) == (d == 0) else n - 1 - n // 2

        def ring(n, i, d, k):
            return lax.rem(i + (k if d == 0 else n - k), n)

        def forward(n, i, peer, ref, blk, sub, s_sem, r_sem, b, h):
            for d in range(2):
                if h > hops(n, b, d):
                    continue
                _, dev = peer(1 if d == 0 else n - 1)
                origin = ring(n, i, 1 - d, h - 1)
                here = rows(ref, origin * blk + b * sub, sub)
                c = copy(here, here, s_sem.at[b, d, h], r_sem.at[b, origin], dev)
                if h > 1:
                    c.wait_recv()
                c.start()
                sends.append(c)

        def settle(n, i, peer, ref, blk, sub, s_sem, r_sem, b):
            for k in range(1, n):
                j, dev = peer(k)
                d = 1 if k <= hops(n, b, 1) else 0
                if (k if d == 1 else n - k) < hops(n, b, d):
                    continue
                here = rows(ref, j * blk + b * sub, sub)
                copy(here, here, s_sem.at[b, 0, 1], r_sem.at[b, j], dev).wait_recv()

        first = (n1, i1, peer1, qg1, CH, CH // 2, a1_s, a1_r)
        second = (n2, i2, peer2, qg2, blk, sub, a2_s, a2_r)
        if cc == 0:
            pq[0] = produce(0)
        else:
            to_partner(produce(0))
            incoming()
            pq[1] = produce(1)
        gather_chunk()
        qg1[pl.ds(pl.multiple_of(i1 * CH, 16), CH), :] = ck[...]
        for b in range(2):
            forward(*first, b, 1)
        if cc == 0:
            incoming()
            to_partner(produce(1))
        for h in range(2, n1 // 2 + 1):
            for b in range(2):
                forward(*first, b, h)

        def pack(b):
            part_rows = CH // 2
            source = jnp.concatenate(
                [qg1[pl.ds(o * CH + b * part_rows, part_rows), :] for o in range(n1)], 0
            )

            def one(r, _):
                sel = onehot(
                    w, n1 * part_rows, lambda i: i // QC * part_rows + r * QC + i % QC
                ).astype(BF)
                here = pl.ds(pl.multiple_of(i2 * blk + b * sub + r * w, 16), w)
                qg2[here, :] = dot(sel, source).astype(BF)
                return 0

            lax.fori_loop(0, RB, one, 0)

        for b in range(2):
            settle(*first, b)
            pack(b)
            forward(*second, b, 1)
        for h in range(2, n2 // 2 + 1):
            for b in range(2):
                forward(*second, b, h)
        big = n2 // 2
        copy(kx, ko, p_s.at[0], p_r.at[0], partner).wait_recv()
        if cc == 1:
            load_n.wait()

        st[...] = jnp.full(st.shape, NEG, F32)
        nq = n2 * w

        def attend(r, _):
            q = jnp.concatenate(
                [qg2[pl.ds(pl.multiple_of(o * blk + r * w, 16), w), :] for o in range(n2)], 0
            )
            if cc == 0:
                k_a, k_b = cvm[idx[r, 0]], ko[r]
            else:
                k_a, k_b = ko[r], nvm[r]
            mine = jnp.where(iota(lens_v.shape, 0) == r + cc * R, lens_v[...], 0)
            length = jnp.sum(mine, axis=0, keepdims=True)[:, :1]
            base = (shard - core) * seq
            place = base + lax.broadcasted_iota(jnp.int32, (nq, seq), 1)
            ok_a, ok_b = place < length, place + seq < length
            s_a = jnp.where(ok_a, dot(q, k_a) * scale, NEG)
            s_b = jnp.where(ok_b, dot(q, k_b) * scale, NEG)
            top = jnp.maximum(
                jnp.max(s_a, axis=1, keepdims=True), jnp.max(s_b, axis=1, keepdims=True)
            )
            p_a = jnp.where(ok_a, jnp.exp(s_a - top), 0.0)
            p_b = jnp.where(ok_b, jnp.exp(s_b - top), 0.0)
            total = jnp.sum(p_a, axis=1, keepdims=True) + jnp.sum(p_b, axis=1, keepdims=True)
            summed = dot_t(p_a.astype(BF), k_a[:DL, :]) + dot_t(p_b.astype(BF), k_b[:DL, :])
            some = total > 0.0
            safe = jnp.where(some, total, 1.0)
            value = (summed * (1.0 / safe)).astype(BF)
            lse = jnp.where(some, top + jnp.log(safe), NEG)
            for o in range(n2):
                acc[pl.ds(pl.multiple_of(o * blk + r * w, 16), w), :] = value[o * w : (o + 1) * w]
            b = r // RB
            lane = lax.broadcasted_iota(jnp.int32, (nq, 128), 1)
            st[b] = jnp.where(lane == r, lse, st[b])
            return 0

        def slot(b, d, h):
            return b * (n2 - 1) + (0 if d == 0 else hops(n2, b, 0)) + h - 1

        def merge(b, target, slots):
            here = pl.ds(pl.multiple_of(target * w, 16), w)
            parts = [st[b, here, :]] + [rss[s * w : (s + 1) * w, :] for s in slots]
            top = functools.reduce(jnp.maximum, parts)
            weights = [jnp.exp(p - top) for p in parts]
            total = functools.reduce(jnp.add, weights)
            weights = [v / total for v in weights]
            st[b, here, :] = top + jnp.log(total)
            lane = lax.broadcasted_iota(jnp.int32, (w, 128), 1)

            def one(r, _):
                mine = pl.ds(pl.multiple_of(target * blk + b * sub + r * w, 16), w)
                values = [acc[mine, :]]
                for s in slots:
                    values.append(rsr[pl.ds(pl.multiple_of(s * sub + r * w, 16), w), :])
                out = None
                for v, g in zip(values, weights):
                    col = jnp.sum(jnp.where(lane == b * RB + r, g, 0.0), axis=1, keepdims=True)
                    term = v.astype(F32) * col
                    out = term if out is None else out + term
                acc[mine, :] = out.astype(BF)
                return 0

            lax.fori_loop(0, RB, one, 0)

        def reduce_copies(b, d, h, target, dev):
            s = slot(b, d, h)
            big_copy = copy(
                rows(acc, target * blk + b * sub, sub),
                rsr.at[pl.ds(s * sub, sub)],
                c_s.at[b, d, h],
                c_r.at[b, d, h],
                dev,
            )
            small_copy = copy(
                st.at[b, pl.ds(pl.multiple_of(target * w, 16), w)],
                rss.at[pl.ds(s * w, w)],
                d_s.at[b, d, h],
                d_r.at[b, d, h],
                dev,
            )
            return big_copy, small_copy

        def step(b, d, h):
            if h > hops(n2, b, d):
                return
            _, dev = peer2(1 if d == 0 else n2 - 1)
            target = ring(n2, i2, d, hops(n2, b, d) - h + 1)
            if h > 1:
                for c in reduce_copies(b, d, h - 1, target, dev):
                    c.wait_recv()
                merge(b, target, [slot(b, d, h - 1)])
            for c in reduce_copies(b, d, h, target, dev):
                c.start()
                sends.append(c)

        for b in range(2):
            settle(*second, b)
            lax.fori_loop(b * RB, (b + 1) * RB, attend, 0)
            for d in range(2):
                step(b, d, 1)
        for h in range(2, big + 1):
            for b in range(2):
                for d in range(2):
                    step(b, d, h)
        for b in range(2):
            slots = []
            for d in range(2):
                last = hops(n2, b, d)
                if last:
                    _, dev = peer2(1 if d == 0 else n2 - 1)
                    for c in reduce_copies(b, d, last, i2, dev):
                        c.wait_recv()
                    slots.append(slot(b, d, last))
            if slots:
                merge(b, i2, slots)

        here = pl.ds(pl.multiple_of(i2 * w, 16), w)
        lane = lax.broadcasted_iota(jnp.int32, (w, 128), 1)
        stm[:w, :] = jnp.where(lane < RB, st[0, here, :], st[1, here, :])
        block = pl.ds(pl.multiple_of(i2 * blk, 16), blk)
        for k in range(1, n1 + 1):
            j, dev = peer1(k)
            sel = onehot(CH, blk, lambda i: i // QC * w + j * QC + i % QC).astype(BF)
            value = dot(sel, acc[block, :]).astype(BF)
            sel = onehot(16, w, lambda i: jnp.where(i < QC, j * QC + i, -1))
            stat = dot(sel, stm[:w, :], precision=lax.Precision.HIGHEST)
            if k == n1:
                rb[pl.ds(pl.multiple_of(i1 * CH, 16), CH), :] = value
                rst[pl.ds(pl.multiple_of(i1 * 16, 16), 16), :] = stat
            else:
                sb[k] = value
                sst[k] = stat
                for c in (
                    copy(sb.at[k], rows(rb, i1 * CH, CH), e_s.at[k], e_r.at[i1], dev),
                    copy(sst.at[k], rows(rst, i1 * 16, 16), f_s.at[k], f_r.at[i1], dev),
                ):
                    c.start()
                    sends.append(c)
        for k in range(1, n1):
            j, dev = peer1(k)
            copy(sb.at[k], rows(rb, j * CH, CH), e_s.at[k], e_r.at[j], dev).wait_recv()
            copy(sst.at[k], rows(rst, j * 16, 16), f_s.at[k], f_r.at[j], dev).wait_recv()

        if cc == 0:
            nkv = dot(sels[...], nkv_ref[...]).astype(BF)
        else:
            mine = onehot(M, M, lambda i: jnp.where(i < RT, i + RT, -1)).astype(BF)
            mine = dot(mine, pick[...]).astype(BF)
            nkv = dot(mine, yrecv[:, QL : QL + KD]).astype(BF)
        fresh = dot_t(ck[...], nkv) * scale
        i = lax.broadcasted_iota(jnp.int32, (CH, M), 0)
        j = lax.broadcasted_iota(jnp.int32, (CH, M), 1)
        seen = (i // QC == j // T) & (j % T <= i % QC // (2 * HL)) & (j < RT)
        fresh = jnp.where(seen, fresh, NEG)
        fill = onehot(CH, 16, lambda i: i % QC)
        own_row = lax.broadcasted_iota(jnp.int32, (CH, 128), 0) // QC
        lane = lax.broadcasted_iota(jnp.int32, (CH, 128), 1)
        lses = []
        for s in range(n1):
            spread_out = dot(fill, rst[s * 16 : (s + 1) * 16, :], precision=lax.Precision.HIGHEST)
            lses.append(
                jnp.sum(jnp.where(lane == own_row, spread_out, 0.0), axis=1, keepdims=True)
            )
        top = functools.reduce(jnp.maximum, lses, jnp.max(fresh, axis=1, keepdims=True))
        probs = jnp.where(seen, jnp.exp(fresh - top), 0.0)
        total = jnp.sum(probs, axis=1, keepdims=True)
        summed = dot(probs.astype(BF), nkv[:, :DL])
        for s in range(n1):
            g = jnp.exp(lses[s] - top)
            total = total + g
            summed = summed + rb[s * CH : (s + 1) * CH, :].astype(F32) * g
        lat[...] = (summed / total).astype(BF)
        for c in sends:
            c.wait_send()

    @pl.when(core == 0)
    def _():
        spread(0, NX, x, x_peer, NZ, z, z_peer)

    @pl.when(core == 1)
    def _():
        spread(1, NZ, z, z_peer, NX, x, x_peer)

    def heads_of(cc):
        sel = onehot(
            HL * RT,
            CH,
            lambda i: i % RT // T * QC + i % T * (2 * HL) + cc * HL + i // RT,
        ).astype(BF)
        return dot(sel, lat[...]).astype(BF)

    fl[...] = heads_of(1 - core)
    swap = copy(fl, lo.at[core], p_s.at[2], p_r.at[2], partner)
    swap.start()
    done.append(swap)
    lo[core] = heads_of(core)
    copy(fl, lo.at[1 - core], p_s.at[2], p_r.at[2], partner).wait_recv()
    every = lo[...].reshape(2 * HL * RT, DL)
    flat = []
    for h in range(HL):
        value = dot(every, wuv_ref[h]).astype(BF)
        sel = onehot(M, 2 * HL * RT, lambda i: i // RT * (HL * RT) + h * RT + i % RT).astype(BF)
        flat.append(dot(sel, value).astype(BF))
    flat = jnp.concatenate(flat, 1)
    load_o.wait()
    part[...] = dot(flat, wov[...])
    shards = 2 * NX * NZ
    for s in range(shards):
        s_pre, rest = divmod(s, 2 * NZL * NX)
        s_x, rest = divmod(rest, 2 * NZL)
        s_zl, s_core = divmod(rest, 2)
        first = s * W // 128
        off = s * W - first * 128
        if off + W <= 128:
            piece = part[:, first * 128 : (first + 1) * 128]
            if off:
                piece = pltpu.roll(piece, 128 - off, 1)
        else:
            piece = pltpu.roll(part[:, first * 128 : (first + 2) * 128], 256 - off, 1)[:, :128]
        po[s_core, s_x, s_pre * NZL + s_zl] = piece
    swap = copy(po.at[1 - core], pr, p_s.at[3], p_r.at[3], partner)
    swap.start()
    done.append(swap)
    swap.wait_recv()
    po[core] = po[core] + pr[...]
    halves = NZ // 2

    def x_hops(b, d):
        return NX // 2 if (b == 0) == (d == 0) else NX - 1 - NX // 2

    def x_slot(b, d, h):
        return b * (NX - 1) + (0 if d == 0 else x_hops(b, 0)) + h - 1

    def x_copy(b, d, h, target):
        _, dev = x_peer(1 if d == 0 else NX - 1)
        return copy(
            po.at[core, target, pl.ds(b * halves, halves)],
            xr.at[x_slot(b, d, h)],
            x_s.at[b, d, h],
            x_r.at[b, d, h],
            dev,
        )

    for h in range(1, NX // 2 + 1):
        for b in range(2):
            for d in range(2):
                if h > x_hops(b, d):
                    continue
                ahead = x_hops(b, d) - h + 1
                target = lax.rem(x + (ahead if d == 0 else NX - ahead), NX)
                if h > 1:
                    x_copy(b, d, h - 1, target).wait_recv()
                    span = pl.ds(b * halves, halves)
                    po[core, target, span] = po[core, target, span] + xr[x_slot(b, d, h - 1)]
                c = x_copy(b, d, h, target)
                c.start()
                done.append(c)
    for b in range(2):
        span = pl.ds(b * halves, halves)
        total = po[core, x, span]
        for d in range(2):
            last = x_hops(b, d)
            if last:
                x_copy(b, d, last, x).wait_recv()
                total = total + xr[x_slot(b, d, last)]
        zs[b * halves : (b + 1) * halves] = total
    for k in range(1, NZ):
        j, dev = z_peer(k)
        c = copy(zs.at[j], zr.at[z], z_s.at[k], z_r.at[z], dev)
        c.start()
        done.append(c)
    total = zs[z]
    for k in range(1, NZ):
        j, dev = z_peer(k)
        copy(zs.at[j], zr.at[j], z_s.at[k], z_r.at[j], dev).wait_recv()
        total = total + zr[j]
    final = total.astype(BF)
    yos[...] = dot_c(pick[...], final).astype(BF)
    for k in range(1, G):
        gg, dev = g_peer(k)
        c = copy(rows(yos, gg * YP, YP), rows(yor, grp * YP, YP), o_s.at[k], o_r.at[grp], dev)
        c.start()
        done.append(c)
    yor[own, :] = yos[own, :]
    for k in range(1, G):
        gg, dev = g_peer(k)
        copy(
            rows(yos, gg * YP, YP), rows(yor, gg * YP, YP), o_s.at[k], o_r.at[gg], dev
        ).wait_recv()
    placed = dot_c(sels[...], final) + dot_c(sely[...], yor[...])
    out_ref[...] = placed[:, :W].astype(BF)
    for c in done:
        c.wait_send()


def local(sizes, cache, cache_len, new_latent, prompt_len, dest, q_latent, new_kv, w_uq, w_uk, w_uv, w_o):
    G, NX, NZ, NZL = sizes
    rows_n, seq, KD = cache.shape
    T, _, QL = q_latent.shape
    HL, DN, DL = w_uk.shape
    DR = KD - DL
    R = new_latent.shape[0]
    PERG = R // G
    YP = up(PERG * T, 16)
    shards = 2 * NX * NZ
    W = w_o.shape[1] // shards
    M = 2 * R * T
    HM = up(R * T, 16)
    QC = T * 2 * HL
    CH = R * QC
    nq = NX * NZ * QC
    KP = up(KD, 128)
    half = DR // 2
    freq = ROPE_BASE ** (-jnp.arange(half, dtype=F32) / half)
    freq = jnp.concatenate([freq, freq])[None, :]
    dims = (G, NX, NZ, NZL, T, R, HL, PERG, YP, KD, DL, DN, DR, QL, W, rows_n)
    tall = max(NX, NZ)

    def slots_rows(n1, n2, per):
        return 2 * (n2 - 1) * n1 * QC * per

    rsr_rows = max(slots_rows(NX, NZ, R // 2), slots_rows(NZ, NX, R // 2), 16)
    rss_rows = max(slots_rows(NX, NZ, 1), slots_rows(NZ, NX, 1), 16)
    hop = tall // 2 + 1
    vmem = pl.BlockSpec(memory_space=pltpu.VMEM)
    anywhere = pl.BlockSpec(memory_space=pl.ANY)
    dma = pltpu.SemaphoreType.DMA
    V = pltpu.VMEM
    out = pl.pallas_call(
        functools.partial(kernel, dims),
        out_shape=jax.ShapeDtypeStruct((T * rows_n, W), BF),
        in_specs=[vmem] * 9 + [anywhere] * 3,
        out_specs=vmem,
        scratch_shapes=[
            V((rows_n, KD, seq), BF),
            V((R, KD, seq), BF),
            V(w_o.shape, BF),
            V((2 * R, 128), jnp.int32),
            pltpu.SMEM((2 * R, 128), jnp.int32),
            V((2 * R, 128), jnp.int32),
            V((M, T * rows_n), BF),
            V((G * YP, T * rows_n), BF),
            V((M, G * YP), BF),
            V((G * YP, QL + KP), BF),
            V((G * YP, QL + KP), BF),
            V((R, KD, seq), BF),
            V((R, KD, seq), BF),
            V((HL, HM, KD), BF),
            V((HL * R * T, KD), BF),
            V((2, HL * R * T, KD), BF),
            V((CH, KD), BF),
            V((tall * CH, KD), BF),
            V((R * nq, KD), BF),
            V((R * nq, DL), BF),
            V((rsr_rows, DL), BF),
            V((2, nq, 128), F32),
            V((rss_rows, 128), F32),
            V((tall * QC, 128), F32),
            V((tall, CH, DL), BF),
            V((tall, 16, 128), F32),
            V((tall * CH, DL), BF),
            V((tall * 16, 128), F32),
            V((CH, DL), BF),
            V((2, HL * R * T, DL), BF),
            V((HL * R * T, DL), BF),
            V((M, shards * W), F32),
            V((2, NX, NZ, M, 128), F32),
            V((NX, NZ, M, 128), F32),
            V((2 * max(NX - 1, 1), NZ // 2, M, 128), F32),
            V((NZ, M, 128), F32),
            V((NZ, M, 128), F32),
            V((G * YP, 128), BF),
            V((G * YP, 128), BF),
            dma((4,)), dma((G,)), dma((G,)), dma((4,)), dma((4,)),
            dma((2, 2, hop)), dma((2, tall)), dma((2, 2, hop)), dma((2, tall)),
            dma((2, 2, hop)), dma((2, 2, hop)), dma((2, 2, hop)), dma((2, 2, hop)),
            dma((tall,)), dma((tall,)), dma((tall,)), dma((tall,)),
            dma((2, 2, hop)), dma((2, 2, hop)), dma((NZ,)), dma((NZ,)), dma((G,)), dma((G,)),
        ],
        compiler_params=pltpu.CompilerParams(
            collective_id=0, has_side_effects=True, vmem_limit_bytes=60 * 2**20
        ),
    )(
        dest.T,
        cache_len[None, :],
        prompt_len[None, :],
        freq,
        q_latent.reshape(T * rows_n, QL),
        new_kv.reshape(T * rows_n, KD),
        w_uq,
        w_uk,
        w_uv,
        cache.transpose(0, 2, 1),
        new_latent.transpose(0, 2, 1),
        w_o,
    )
    return out.reshape(T, rows_n, W)


def solution(mesh):
    placed = (
        P("grp", ("pre", "dec"), None),
        P("grp"),
        P("grp", ("pre", "dec"), None),
        P(),
        P(),
        P(None, "grp", None),
        P(None, "grp", None),
        P(None, ("pre", "dec")),
        P(("pre", "dec"), None, None),
        P(("pre", "dec"), None, None),
        P(("pre", "dec"), None),
    )
    zl = 2
    sizes = (
        mesh.shape["grp"],
        mesh.shape["dec"] // (2 * zl),
        mesh.shape["pre"] * zl,
        zl,
    )
    return jax.shard_map(
        functools.partial(local, sizes),
        mesh=mesh,
        in_specs=placed,
        out_specs=P(None, "grp", ("pre", "dec")),
        check_vma=False,
    )
```

time: 899 us -> 116 us (0.13)
  waiting for transfers between devices: 754 us -> 0 us
  Pallas kernels: 0 us -> 114 us
  local copies, waits for them, and re-layouts: 64.3 us -> 1.31 us
  matrix products: 32.6 us -> 0 us
  starting transfers between devices: 24.3 us -> 0 us
  between operations: 13.4 us -> 0.01 us
  other arithmetic: 10.1 us -> 0.6 us
    all_to_all x3 -> x0, waiting for transfers between devices: 276 us -> none  [the longest x1 270 us: local(): lax.all_to_all(local_acc[None], ('pre', 'dec'), split_axis=3, concat_axis...]
    unnamed x4 -> x0, waiting for transfers between devices: 266 us -> none
    all_gather x2 -> x0, waiting for transfers between devices: 211 us -> none  [the longest x1 113 us: local(): all_query = lax.all_gather(query, ('pre', 'dec'), axis=2, tiled=True)]
    pallas_call x0 -> x1, Pallas kernels: none -> 114 us  [local(): pl.pallas_call(functools.partial(kernel, dims), out_shape=jax.ShapeDtypeS...]
    dot_general x9 -> x0, matrix products: 32.6 us -> none  [the longest x1 10.4 us: local(): jnp.einsum('kr,ksc->rsc', select.astype(jnp.bfloat16), arrived, preferred...]
    unnamed x29 -> x1, local copies, waits for them, and re-layouts: 32.9 us -> 1.31 us
    all_to_all x3 -> x0, starting transfers between devices: 24.1 us -> none  [the longest x1 10.7 us: local(): lax.all_to_all(local_acc[None], ('pre', 'dec'), split_axis=3, concat_axis...]
    broadcast_in_dim x3 -> x0, local copies, waits for them, and re-layouts: 14.3 us -> none  [the longest x1 12.7 us: local(): local_acc[None]]
  transfers between devices with their start and end apart: 6 -> 0, of which waited for: 5 -> 0; matrix products, arithmetic and copies ran while one was open for 5% -> 0% of each run, Pallas kernels for 0% -> 0%
where the time goes in v1:
time: 116 us
  Pallas kernels  114 us (98%)
  local copies, waits for them, and re-layouts  1.31 us (1%)
    pallas_call x1, Pallas kernels, local(): pl.pallas_call(functools.partial(kernel, dims), out_shape=jax.ShapeDtypeS...  114 us

profile of v1, /device:TPU:8, one launch (start us, length us, event | category | flops | bytes accessed | tf_op | source)
XLA Modules:
  0.0 116.3 jit_solution(11983175971093768273)
XLA Ops:
  0.0 0.6 maximum_bitcast_fusion.freq_ref
  0.6 114.4 %shard_map.109 = bf16[48,112]{1,0:T(8,128)(2,1)} custom-call(s32[2,32]{1,0:T(2,128)} %bitcast.15, s32[1,16]{1,0:T(1,128)} %bitcast.16, s32[1,32]{1,0:T(1,128)} %bitcast.17, f32[1,64]{1,0:T(1,128)} %maximum_bitcast_fusion.freq_ref, bf16[48,1536]{1,0:T(8,128)(2,1)} %bitcast.12, bf16[48,576]{1,0:T(8,128)(2,1)} %bitcast.13, bf16[1536,384]{1,0:T(8,128)(2,1)} %wuq_ref.1, ...), custom_call_target="tpu_custom_call" | custom-call | tf_op jit(solution)/shard_map/pallas_call | solution.py:667
  115.0 1.3 %copy.13 = bf16[3,16,112]{2,1,0:T(8,128)(2,1)} copy(bf16[3,16,112]{2,1,0:T(8,128)(2,1)} %bitcast.14) | data formatting | bytes 21504
  (1 shorter events, 0.0 us)

commit v2 on v1

--- a/solution.py
+++ b/solution.py
@@ -42,20 +42,21 @@
     dest_ref, clen_ref, plen_ref, freq_ref, ql_ref, nkv_ref, wuq_ref, wuk_ref, wuv_ref,
     cache_ref, newl_ref, wo_ref,
     out_ref,
-    cvm, nvm, wov, idx_v, idx, lens_v, sels, sely, pick,
-    ysend, yrecv, kx, ko, qh, qsend, pq, ck, qg1, qg2, acc, rsr, st, rss, stm,
-    sb, sst, rb, rst, lat, lo, fl, part, po, pr, xr, zs, zr, yos, yor,
+    cvm, nvm, wov, idx_v, idx, lens_v, sels, sely, selh, pick, xlo, xhi,
+    ysend, yrecv, kx, ko, qh, qsend, pq, ck, qall, qp, acc, rsr, st, rss,
+    sb, sst, rb, rst, lat, lo, fl, part, po, pr, xs, xr, zs, zr, yos, yor,
     l_s, y_s, y_r, p_s, p_r, a1_s, a1_r, a2_s, a2_r, c_s, c_r, d_s, d_r,
     e_s, e_r, f_s, f_r, x_s, x_r, z_s, z_r, o_s, o_r,
 ):
-    G, NX, NZ, NZL, T, R, HL, PERG, YP, KD, DL, DN, DR, QL, W, SLOTS = dims
+    G, NX, NZ, NZL, T, R, HL, PERG, YP, KD, DL, DN, DR, QL, W, SLOTS, QA = dims
     QC = T * 2 * HL
     CH = R * QC
     RT = R * T
     M = 2 * RT
     HM = up(RT, 16)
     RB = R // 2
-    KP = up(KD, 128)
+    RQ = R // 4
+    QB = QL - QA
     NEW = G * R
     TS = T * SLOTS
     PT = PERG * T
@@ -149,55 +150,41 @@
     ).astype(BF)
     i, j = iota((G * YP, NEW), 0), iota((G * YP, NEW), 1)
     u = i % YP
-    from_k = jnp.where((j // R == i // YP) & here_row & (rank_row == u // T) & (u < PT), 1.0, 0.0)
+    from_k = jnp.where((j // R == i // YP) & here_row & (rank_row == u % PT // T), 1.0, 0.0)
     to_slot = jnp.where(spot_col == iota((NEW, TS), 1) % SLOTS, 1.0, 0.0)
     i, j = iota((G * YP, TS), 0), iota((G * YP, TS), 1)
-    sely[...] = jnp.where(
-        j // SLOTS == i % YP % T, dot(from_k.astype(BF), to_slot.astype(BF)), 0.0
-    ).astype(BF)
+    u = i % YP
+    chosen = dot(from_k.astype(BF), to_slot.astype(BF))
+    chosen = jnp.where(j // SLOTS == u % PT % T, chosen, 0.0)
+    sely[...] = jnp.where(u < PT, chosen, 0.0).astype(BF)
+    selh[...] = jnp.where((u >= PT) & (u < 2 * PT), chosen, 0.0).astype(BF)
     i, j = iota((M, NEW), 0), iota((M, NEW), 1)
     own_k = (j == (i - RT) // T + grp * R) & (i >= RT)
     key_col = jnp.sum(jnp.where(own_k, to_row * YP + rank_row * T, 0), axis=1, keepdims=True)
     i, j = iota((M, G * YP), 0), iota((M, G * YP), 1)
     pick[...] = jnp.where((key_col + i % T == j) & (i >= RT), 1.0, 0.0).astype(BF)
-    ysend[:, :QL] = dot(sely[...], ql_ref[...]).astype(BF)
-    ysend[:, QL : QL + KD] = dot(sely[...], nkv_ref[...]).astype(BF)
-
-    pl.semaphore_wait(barrier, len(peers))
-    done = []
-    for k in range(1, G):
-        gg, dev = g_peer(k)
-        c = copy(rows(ysend, gg * YP, YP), rows(yrecv, grp * YP, YP), y_s.at[k], y_r.at[grp], dev)
-        c.start()
-        done.append(c)
-    own = pl.ds(pl.multiple_of(grp * YP, 16), YP)
-    yrecv[own, :] = ysend[own, :]
-
-    keys = copy(kx, ko, p_s.at[0], p_r.at[0], partner)
-    done.append(keys)
-
-    @pl.when(core == 0)
-    def _():
-        copy(newl_ref, ko, p_s.at[0], p_r.at[0], partner).start()
-
-    fetch.wait()
-    load_c.wait()
-
-    @pl.when(core == 1)
-    def _():
-        for j in range(R):
-            kx[j] = cvm[idx[j, 0]]
-        keys.start()
-        load_n.start()
-
-    load_o.start()
-
+    xlo[...] = jnp.zeros(xlo.shape, BF)
+    xhi[...] = jnp.zeros(xhi.shape, BF)
+    xlo[:, :QA] = ql_ref[:, :QA]
+    if QB:
+        xhi[:, :QB] = ql_ref[:, QA:]
+    xhi[:, QB : QB + KD] = nkv_ref[...]
+    ysend[...] = (dot(sely[...], xlo[...]) + dot(selh[...], xhi[...])).astype(BF)
     half_dr = DR // 2
     lens_row = jnp.sum(
         jnp.where(iota((2 * R, 2 * R), 0) == iota((2 * R, 2 * R), 1), lens_col, 0),
         axis=0,
         keepdims=True,
     )
+
+    def fresh_rows(count):
+        i, j = iota((count, M), 0), iota((count, M), 1)
+        low = jnp.where((j == i + RT) & (i < RT), 1.0, 0.0).astype(BF)
+        low = dot(low, pick[...]).astype(BF)
+        size = G * YP
+        i, j = iota((size, size), 0), iota((size, size), 1)
+        down = jnp.where(j == i + PT, 1.0, 0.0).astype(BF)
+        return low, dot(low, down).astype(BF)
 
     def produce(half):
         i = iota((HM, 2 * R), 0)
@@ -208,11 +195,13 @@
         sin = jnp.where(iota((HM, DR), 1) < half_dr, -sin, sin)
         if half == 0:
             xin = dot(sels[:HM, :], ql_ref[...]).astype(BF)
+            qf = dot(xin, wuq_ref[...])
         else:
-            i = iota((HM, M), 0)
-            low = jnp.where((iota((HM, M), 1) == i + RT) & (i < RT), 1.0, 0.0).astype(BF)
-            xin = dot(dot(low, pick[...]).astype(BF), yrecv[:, :QL]).astype(BF)
-        qf = dot(xin, wuq_ref[...]).astype(BF)
+            low, high = fresh_rows(HM)
+            qf = dot(dot(low, yrecv[:, :QA]).astype(BF), wuq_ref[:QA, :])
+            if QB:
+                qf = qf + dot(dot(high, yrecv[:, :QB]).astype(BF), wuq_ref[QA:, :])
+        qf = qf.astype(BF)
         HD = DN + DR
         for h in range(HL):
             nope = dot(qf, onehot(HL * HD, DN, lambda i: i - h * HD).astype(BF)).astype(BF)
@@ -234,6 +223,35 @@
             total = term if total is None else total + term
         return total.astype(BF)
 
+    pl.semaphore_wait(barrier, len(peers))
+    done = []
+    for k in range(1, G):
+        gg, dev = g_peer(k)
+        c = copy(rows(ysend, gg * YP, YP), rows(yrecv, grp * YP, YP), y_s.at[k], y_r.at[grp], dev)
+        c.start()
+        done.append(c)
+    own = pl.ds(pl.multiple_of(grp * YP, 16), YP)
+    yrecv[own, :] = ysend[own, :]
+
+    keys = copy(kx, ko, p_s.at[0], p_r.at[0], partner)
+    done.append(keys)
+
+    @pl.when(core == 0)
+    def _():
+        copy(newl_ref, ko, p_s.at[0], p_r.at[0], partner).start()
+
+    fetch.wait()
+    load_c.wait()
+
+    @pl.when(core == 1)
+    def _():
+        for j in range(R):
+            kx[j] = cvm[idx[j, 0]]
+        keys.start()
+        load_n.start()
+
+    load_o.start()
+
     def incoming():
         for k in range(1, G):
             gg, dev = g_peer(k)
@@ -258,7 +276,7 @@
     def spread(cc, n1, i1, peer1, n2, i2, peer2):
         w = n1 * QC
         blk = R * w
-        sub = RB * w
+        sub = RQ * w
         sends = []
 
         def hops(n, b, d):
@@ -267,30 +285,67 @@
         def ring(n, i, d, k):
             return lax.rem(i + (k if d == 0 else n - k), n)
 
-        def forward(n, i, peer, ref, blk, sub, s_sem, r_sem, b, h):
-            for d in range(2):
-                if h > hops(n, b, d):
+        part_rows = CH // 2
+
+        def cell(o2, o1, b):
+            return rows(qall, (o2 * n1 + o1) * CH + b * part_rows, part_rows)
+
+        def new_at(s):
+            if s == 0:
+                return [(b, i1, None) for b in range(2)]
+            return [
+                (b, ring(n1, i1, 1 - d, s), d)
+                for b in range(2)
+                for d in range(2)
+                if s <= hops(n1, b, d)
+            ]
+
+        def first_copy(b, o1, d, h):
+            _, dev = peer1(1 if d == 0 else n1 - 1)
+            here = cell(i2, o1, b)
+            return copy(here, here, a1_s.at[b, d, h], a1_r.at[b, o1], dev)
+
+        def second_copy(b, o1, o2, d, h):
+            _, dev = peer2(1 if d == 0 else n2 - 1)
+            here = cell(o2, o1, b)
+            return copy(here, here, a2_s.at[b, o1, d, h], a2_r.at[b, o1, o2], dev)
+
+        def launch(c):
+            c.start()
+            sends.append(c)
+
+        def gather_step(s):
+            if s <= n1 // 2:
+                for b, o1, d in new_at(s):
+                    if s:
+                        first_copy(b, o1, d, s).wait_recv()
+                    for way in (0, 1) if d is None else (d,):
+                        if s + 1 <= hops(n1, b, way):
+                            launch(first_copy(b, o1, way, s + 1))
+                    for way in range(2):
+                        if hops(n2, b, way):
+                            launch(second_copy(b, o1, i2, way, 1))
+            for h in range(2, n2 // 2 + 1):
+                if not 0 <= s - h + 1 <= n1 // 2:
                     continue
-                _, dev = peer(1 if d == 0 else n - 1)
-                origin = ring(n, i, 1 - d, h - 1)
-                here = rows(ref, origin * blk + b * sub, sub)
-                c = copy(here, here, s_sem.at[b, d, h], r_sem.at[b, origin], dev)
-                if h > 1:
-                    c.wait_recv()
-                c.start()
-                sends.append(c)
-
-        def settle(n, i, peer, ref, blk, sub, s_sem, r_sem, b):
-            for k in range(1, n):
-                j, dev = peer(k)
-                d = 1 if k <= hops(n, b, 1) else 0
-                if (k if d == 1 else n - k) < hops(n, b, d):
-                    continue
-                here = rows(ref, j * blk + b * sub, sub)
-                copy(here, here, s_sem.at[b, 0, 1], r_sem.at[b, j], dev).wait_recv()
-
-        first = (n1, i1, peer1, qg1, CH, CH // 2, a1_s, a1_r)
-        second = (n2, i2, peer2, qg2, blk, sub, a2_s, a2_r)
+                for b, o1, _ in new_at(s - h + 1):
+                    for way in range(2):
+                        if h <= hops(n2, b, way):
+                            o2 = ring(n2, i2, 1 - way, h - 1)
+                            c = second_copy(b, o1, o2, way, h)
+                            c.wait_recv()
+                            launch(c)
+
+        def settle(b):
+            for k1 in range(n1):
+                o1 = lax.rem(i1 + k1, n1)
+                for k2 in range(1, n2):
+                    o2 = lax.rem(i2 + k2, n2)
+                    way = 1 if k2 <= hops(n2, b, 1) else 0
+                    dist = k2 if way == 1 else n2 - k2
+                    if dist == hops(n2, b, way):
+                        second_copy(b, o1, o2, way, dist).wait_recv()
+
         if cc == 0:
             pq[0] = produce(0)
         else:
@@ -298,51 +353,53 @@
             incoming()
             pq[1] = produce(1)
         gather_chunk()
-        qg1[pl.ds(pl.multiple_of(i1 * CH, 16), CH), :] = ck[...]
-        for b in range(2):
-            forward(*first, b, 1)
+        qall[pl.ds(pl.multiple_of((i2 * n1 + i1) * CH, 16), CH), :] = ck[...]
+        gather_step(0)
         if cc == 0:
             incoming()
             to_partner(produce(1))
-        for h in range(2, n1 // 2 + 1):
-            for b in range(2):
-                forward(*first, b, h)
+        for s in range(1, n1 // 2 + max(1, n2 // 2)):
+            gather_step(s)
+
+        many = min(4, n1)
+        span = many * QC
+        mix = onehot(
+            RB * span,
+            RB * span,
+            lambda i: i % span // QC * part_rows + i // span * QC + i % QC,
+        ).astype(BF)
 
         def pack(b):
-            part_rows = CH // 2
-            source = jnp.concatenate(
-                [qg1[pl.ds(o * CH + b * part_rows, part_rows), :] for o in range(n1)], 0
-            )
-
-            def one(r, _):
-                sel = onehot(
-                    w, n1 * part_rows, lambda i: i // QC * part_rows + r * QC + i % QC
-                ).astype(BF)
-                here = pl.ds(pl.multiple_of(i2 * blk + b * sub + r * w, 16), w)
-                qg2[here, :] = dot(sel, source).astype(BF)
+            def one(g, _):
+                source = jnp.concatenate(
+                    [
+                        qall[
+                            pl.ds(
+                                pl.multiple_of((g * many + o) * CH + b * part_rows, 16), part_rows
+                            ),
+                            :,
+                        ]
+                        for o in range(many)
+                    ],
+                    0,
+                )
+                mixed = dot(mix, source).astype(BF)
+                for r in range(RB):
+                    here = pl.ds(pl.multiple_of(r * nq + g * span, 8), span)
+                    qp[here, :] = mixed[r * span : (r + 1) * span]
                 return 0
 
-            lax.fori_loop(0, RB, one, 0)
-
-        for b in range(2):
-            settle(*first, b)
-            pack(b)
-            forward(*second, b, 1)
-        for h in range(2, n2 // 2 + 1):
-            for b in range(2):
-                forward(*second, b, h)
+            lax.fori_loop(0, n1 * n2 // many, one, 0)
+
+        nq = n2 * w
         big = n2 // 2
         copy(kx, ko, p_s.at[0], p_r.at[0], partner).wait_recv()
         if cc == 1:
             load_n.wait()
 
         st[...] = jnp.full(st.shape, NEG, F32)
-        nq = n2 * w
-
         def attend(r, _):
-            q = jnp.concatenate(
-                [qg2[pl.ds(pl.multiple_of(o * blk + r * w, 16), w), :] for o in range(n2)], 0
-            )
+            q = qp[pl.ds(pl.multiple_of(lax.rem(r, RB) * nq, 16), nq), :]
             if cc == 0:
                 k_a, k_b = cvm[idx[r, 0]], ko[r]
             else:
@@ -367,137 +424,144 @@
             lse = jnp.where(some, top + jnp.log(safe), NEG)
             for o in range(n2):
                 acc[pl.ds(pl.multiple_of(o * blk + r * w, 16), w), :] = value[o * w : (o + 1) * w]
-            b = r // RB
-            lane = lax.broadcasted_iota(jnp.int32, (nq, 128), 1)
-            st[b] = jnp.where(lane == r, lse, st[b])
+                column = jnp.where(iota((w, 128), 0) == iota((w, 128), 1), lse[o * w : (o + 1) * w], 0.0)
+                line = jnp.sum(column, axis=0, keepdims=True)
+                st[r // RQ, o] = jnp.where(iota((R, 128), 0) == r, line, st[r // RQ, o])
             return 0
 
-        def slot(b, d, h):
-            return b * (n2 - 1) + (0 if d == 0 else hops(n2, b, 0)) + h - 1
-
-        def merge(b, target, slots):
-            here = pl.ds(pl.multiple_of(target * w, 16), w)
-            parts = [st[b, here, :]] + [rss[s * w : (s + 1) * w, :] for s in slots]
+        def slot(q, d, h):
+            return q * (n2 - 1) + (0 if d == 0 else hops(n2, q % 2, 0)) + h - 1
+
+        def merge(q, target, slots):
+            parts = [st[q, target]] + [rss[s] for s in slots]
             top = functools.reduce(jnp.maximum, parts)
             weights = [jnp.exp(p - top) for p in parts]
             total = functools.reduce(jnp.add, weights)
             weights = [v / total for v in weights]
-            st[b, here, :] = top + jnp.log(total)
-            lane = lax.broadcasted_iota(jnp.int32, (w, 128), 1)
-
-            def one(r, _):
-                mine = pl.ds(pl.multiple_of(target * blk + b * sub + r * w, 16), w)
+            st[q, target] = top + jnp.log(total)
+            same = iota((w, 128), 0) == iota((w, 128), 1)
+            for r in range(RQ):
+                mine = pl.ds(pl.multiple_of(target * blk + q * sub + r * w, 16), w)
                 values = [acc[mine, :]]
                 for s in slots:
-                    values.append(rsr[pl.ds(pl.multiple_of(s * sub + r * w, 16), w), :])
+                    values.append(rsr[pl.ds(s * sub + r * w, w), :])
                 out = None
+                row = q * RQ + r
                 for v, g in zip(values, weights):
-                    col = jnp.sum(jnp.where(lane == b * RB + r, g, 0.0), axis=1, keepdims=True)
+                    col = jnp.sum(jnp.where(same, g[row : row + 1, :], 0.0), axis=1, keepdims=True)
                     term = v.astype(F32) * col
                     out = term if out is None else out + term
                 acc[mine, :] = out.astype(BF)
-                return 0
-
-            lax.fori_loop(0, RB, one, 0)
-
-        def reduce_copies(b, d, h, target, dev):
-            s = slot(b, d, h)
+
+        def reduce_copies(q, d, h, target, dev):
+            s = slot(q, d, h)
             big_copy = copy(
-                rows(acc, target * blk + b * sub, sub),
+                rows(acc, target * blk + q * sub, sub),
                 rsr.at[pl.ds(s * sub, sub)],
-                c_s.at[b, d, h],
-                c_r.at[b, d, h],
+                c_s.at[q, d, h],
+                c_r.at[q, d, h],
                 dev,
             )
             small_copy = copy(
-                st.at[b, pl.ds(pl.multiple_of(target * w, 16), w)],
-                rss.at[pl.ds(s * w, w)],
-                d_s.at[b, d, h],
-                d_r.at[b, d, h],
-                dev,
+                st.at[q, target], rss.at[s], d_s.at[q, d, h], d_r.at[q, d, h], dev
             )
             return big_copy, small_copy
 
-        def step(b, d, h):
-            if h > hops(n2, b, d):
+        def step(q, d, h):
+            if h > hops(n2, q % 2, d):
                 return
             _, dev = peer2(1 if d == 0 else n2 - 1)
-            target = ring(n2, i2, d, hops(n2, b, d) - h + 1)
+            target = ring(n2, i2, d, hops(n2, q % 2, d) - h + 1)
             if h > 1:
-                for c in reduce_copies(b, d, h - 1, target, dev):
+                for c in reduce_copies(q, d, h - 1, target, dev):
                     c.wait_recv()
-                merge(b, target, [slot(b, d, h - 1)])
-            for c in reduce_copies(b, d, h, target, dev):
-                c.start()
-                sends.append(c)
+                merge(q, target, [slot(q, d, h - 1)])
+            for c in reduce_copies(q, d, h, target, dev):
+                launch(c)
 
         for b in range(2):
-            settle(*second, b)
-            lax.fori_loop(b * RB, (b + 1) * RB, attend, 0)
-            for d in range(2):
-                step(b, d, 1)
+            settle(b)
+            pack(b)
+            for q in (2 * b, 2 * b + 1):
+                lax.fori_loop(q * RQ, (q + 1) * RQ, attend, 0)
+                for d in range(2):
+                    step(q, d, 1)
         for h in range(2, big + 1):
-            for b in range(2):
+            for q in range(4):
                 for d in range(2):
-                    step(b, d, h)
+                    step(q, d, h)
+
         for b in range(2):
-            slots = []
-            for d in range(2):
-                last = hops(n2, b, d)
-                if last:
-                    _, dev = peer2(1 if d == 0 else n2 - 1)
-                    for c in reduce_copies(b, d, last, i2, dev):
-                        c.wait_recv()
-                    slots.append(slot(b, d, last))
-            if slots:
-                merge(b, i2, slots)
-
-        here = pl.ds(pl.multiple_of(i2 * w, 16), w)
-        lane = lax.broadcasted_iota(jnp.int32, (w, 128), 1)
-        stm[:w, :] = jnp.where(lane < RB, st[0, here, :], st[1, here, :])
-        block = pl.ds(pl.multiple_of(i2 * blk, 16), blk)
+            for q in (2 * b, 2 * b + 1):
+                slots = []
+                for d in range(2):
+                    last = hops(n2, q % 2, d)
+                    if last:
+                        _, dev = peer2(1 if d == 0 else n2 - 1)
+                        for c in reduce_copies(q, d, last, i2, dev):
+                            c.wait_recv()
+                        slots.append(slot(q, d, last))
+                if slots:
+                    merge(q, i2, slots)
+            block = pl.ds(pl.multiple_of(i2 * blk + 2 * b * sub, 16), 2 * sub)
+            for k in range(1, n1 + 1):
+                j, dev = peer1(k)
+                sel = onehot(part_rows, 2 * sub, lambda i: i // QC * w + j * QC + i % QC)
+                value = dot(sel.astype(BF), acc[block, :]).astype(BF)
+                if k == n1:
+                    rb[pl.ds(pl.multiple_of(i1 * CH + b * part_rows, 16), part_rows), :] = value
+                    continue
+                sb[k, b * part_rows : (b + 1) * part_rows] = value
+                launch(
+                    copy(
+                        sb.at[k, pl.ds(b * part_rows, part_rows)],
+                        rows(rb, i1 * CH + b * part_rows, part_rows),
+                        e_s.at[k, b],
+                        e_r.at[i1, b],
+                        dev,
+                    )
+                )
+        stats = st[0, i2]
+        for q in range(1, 4):
+            stats = jnp.where(iota((R, 128), 0) // RQ == q, st[q, i2], stats)
         for k in range(1, n1 + 1):
             j, dev = peer1(k)
-            sel = onehot(CH, blk, lambda i: i // QC * w + j * QC + i % QC).astype(BF)
-            value = dot(sel, acc[block, :]).astype(BF)
-            sel = onehot(16, w, lambda i: jnp.where(i < QC, j * QC + i, -1))
-            stat = dot(sel, stm[:w, :], precision=lax.Precision.HIGHEST)
+            sel = onehot(128, 128, lambda i: jnp.where(i // QC == j, i % QC, -1))
+            stat = dot(stats, sel, precision=lax.Precision.HIGHEST)
             if k == n1:
-                rb[pl.ds(pl.multiple_of(i1 * CH, 16), CH), :] = value
-                rst[pl.ds(pl.multiple_of(i1 * 16, 16), 16), :] = stat
-            else:
-                sb[k] = value
-                sst[k] = stat
-                for c in (
-                    copy(sb.at[k], rows(rb, i1 * CH, CH), e_s.at[k], e_r.at[i1], dev),
-                    copy(sst.at[k], rows(rst, i1 * 16, 16), f_s.at[k], f_r.at[i1], dev),
-                ):
-                    c.start()
-                    sends.append(c)
+                rst[i1] = stat
+                continue
+            sst[k] = stat
+            launch(copy(sst.at[k], rst.at[i1], f_s.at[k], f_r.at[i1], dev))
         for k in range(1, n1):
             j, dev = peer1(k)
-            copy(sb.at[k], rows(rb, j * CH, CH), e_s.at[k], e_r.at[j], dev).wait_recv()
-            copy(sst.at[k], rows(rst, j * 16, 16), f_s.at[k], f_r.at[j], dev).wait_recv()
+            for b in range(2):
+                copy(
+                    sb.at[k, pl.ds(b * part_rows, part_rows)],
+                    rows(rb, j * CH + b * part_rows, part_rows),
+                    e_s.at[k, b],
+                    e_r.at[j, b],
+                    dev,
+                ).wait_recv()
+            copy(sst.at[k], rst.at[j], f_s.at[k], f_r.at[j], dev).wait_recv()
 
         if cc == 0:
             nkv = dot(sels[...], nkv_ref[...]).astype(BF)
         else:
-            mine = onehot(M, M, lambda i: jnp.where(i < RT, i + RT, -1)).astype(BF)
-            mine = dot(mine, pick[...]).astype(BF)
-            nkv = dot(mine, yrecv[:, QL : QL + KD]).astype(BF)
+            nkv = dot(fresh_rows(M)[1], yrecv[:, QB : QB + KD]).astype(BF)
         fresh = dot_t(ck[...], nkv) * scale
         i = lax.broadcasted_iota(jnp.int32, (CH, M), 0)
         j = lax.broadcasted_iota(jnp.int32, (CH, M), 1)
         seen = (i // QC == j // T) & (j % T <= i % QC // (2 * HL)) & (j < RT)
         fresh = jnp.where(seen, fresh, NEG)
-        fill = onehot(CH, 16, lambda i: i % QC)
-        own_row = lax.broadcasted_iota(jnp.int32, (CH, 128), 0) // QC
+        fill = onehot(CH, R, lambda i: i // QC)
+        own_head = lax.broadcasted_iota(jnp.int32, (CH, 128), 0) % QC
         lane = lax.broadcasted_iota(jnp.int32, (CH, 128), 1)
         lses = []
         for s in range(n1):
-            spread_out = dot(fill, rst[s * 16 : (s + 1) * 16, :], precision=lax.Precision.HIGHEST)
+            spread_out = dot(fill, rst[s], precision=lax.Precision.HIGHEST)
             lses.append(
-                jnp.sum(jnp.where(lane == own_row, spread_out, 0.0), axis=1, keepdims=True)
+                jnp.sum(jnp.where(lane == own_head, spread_out, 0.0), axis=1, keepdims=True)
             )
         top = functools.reduce(jnp.maximum, lses, jnp.max(fresh, axis=1, keepdims=True))
         probs = jnp.where(seen, jnp.exp(fresh - top), 0.0)
@@ -561,47 +625,18 @@
     done.append(swap)
     swap.wait_recv()
     po[core] = po[core] + pr[...]
-    halves = NZ // 2
-
-    def x_hops(b, d):
-        return NX // 2 if (b == 0) == (d == 0) else NX - 1 - NX // 2
-
-    def x_slot(b, d, h):
-        return b * (NX - 1) + (0 if d == 0 else x_hops(b, 0)) + h - 1
-
-    def x_copy(b, d, h, target):
-        _, dev = x_peer(1 if d == 0 else NX - 1)
-        return copy(
-            po.at[core, target, pl.ds(b * halves, halves)],
-            xr.at[x_slot(b, d, h)],
-            x_s.at[b, d, h],
-            x_r.at[b, d, h],
-            dev,
-        )
-
-    for h in range(1, NX // 2 + 1):
-        for b in range(2):
-            for d in range(2):
-                if h > x_hops(b, d):
-                    continue
-                ahead = x_hops(b, d) - h + 1
-                target = lax.rem(x + (ahead if d == 0 else NX - ahead), NX)
-                if h > 1:
-                    x_copy(b, d, h - 1, target).wait_recv()
-                    span = pl.ds(b * halves, halves)
-                    po[core, target, span] = po[core, target, span] + xr[x_slot(b, d, h - 1)]
-                c = x_copy(b, d, h, target)
-                c.start()
-                done.append(c)
-    for b in range(2):
-        span = pl.ds(b * halves, halves)
-        total = po[core, x, span]
-        for d in range(2):
-            last = x_hops(b, d)
-            if last:
-                x_copy(b, d, last, x).wait_recv()
-                total = total + xr[x_slot(b, d, last)]
-        zs[b * halves : (b + 1) * halves] = total
+    for k in range(1, NX):
+        j, dev = x_peer(k)
+        xs[k] = po[core, j].astype(BF)
+        c = copy(xs.at[k], xr.at[x], x_s.at[k], x_r.at[x], dev)
+        c.start()
+        done.append(c)
+    total = po[core, x]
+    for k in range(1, NX):
+        j, dev = x_peer(k)
+        copy(xs.at[k], xr.at[j], x_s.at[k], x_r.at[j], dev).wait_recv()
+        total = total + xr[j].astype(F32)
+    zs[...] = total
     for k in range(1, NZ):
         j, dev = z_peer(k)
         c = copy(zs.at[j], zr.at[z], z_s.at[k], z_r.at[z], dev)
@@ -639,7 +674,7 @@
     DR = KD - DL
     R = new_latent.shape[0]
     PERG = R // G
-    YP = up(PERG * T, 16)
+    YP = up(2 * PERG * T, 16)
     shards = 2 * NX * NZ
     W = w_o.shape[1] // shards
     M = 2 * R * T
@@ -648,17 +683,18 @@
     CH = R * QC
     nq = NX * NZ * QC
     KP = up(KD, 128)
+    QA = min(QL, up((QL + KP) // 2, 128))
+    YW = max(QA, QL - QA + KP)
     half = DR // 2
     freq = ROPE_BASE ** (-jnp.arange(half, dtype=F32) / half)
     freq = jnp.concatenate([freq, freq])[None, :]
-    dims = (G, NX, NZ, NZL, T, R, HL, PERG, YP, KD, DL, DN, DR, QL, W, rows_n)
+    dims = (G, NX, NZ, NZL, T, R, HL, PERG, YP, KD, DL, DN, DR, QL, W, rows_n, QA)
     tall = max(NX, NZ)
 
     def slots_rows(n1, n2, per):
         return 2 * (n2 - 1) * n1 * QC * per
 
     rsr_rows = max(slots_rows(NX, NZ, R // 2), slots_rows(NZ, NX, R // 2), 16)
-    rss_rows = max(slots_rows(NX, NZ, 1), slots_rows(NZ, NX, 1), 16)
     hop = tall // 2 + 1
     vmem = pl.BlockSpec(memory_space=pltpu.VMEM)
     anywhere = pl.BlockSpec(memory_space=pl.ANY)
@@ -678,42 +714,45 @@
             V((2 * R, 128), jnp.int32),
             V((M, T * rows_n), BF),
             V((G * YP, T * rows_n), BF),
+            V((G * YP, T * rows_n), BF),
             V((M, G * YP), BF),
-            V((G * YP, QL + KP), BF),
-            V((G * YP, QL + KP), BF),
+            V((T * rows_n, YW), BF),
+            V((T * rows_n, YW), BF),
+            V((G * YP, YW), BF),
+            V((G * YP, YW), BF),
             V((R, KD, seq), BF),
             V((R, KD, seq), BF),
             V((HL, HM, KD), BF),
             V((HL * R * T, KD), BF),
             V((2, HL * R * T, KD), BF),
             V((CH, KD), BF),
-            V((tall * CH, KD), BF),
-            V((R * nq, KD), BF),
+            V((NX * NZ * CH, KD), BF),
+            V((R // 2 * nq, KD), BF),
             V((R * nq, DL), BF),
             V((rsr_rows, DL), BF),
-            V((2, nq, 128), F32),
-            V((rss_rows, 128), F32),
-            V((tall * QC, 128), F32),
+            V((4, tall, R, 128), F32),
+            V((4 * (tall - 1), R, 128), F32),
             V((tall, CH, DL), BF),
-            V((tall, 16, 128), F32),
+            V((tall, R, 128), F32),
             V((tall * CH, DL), BF),
-            V((tall * 16, 128), F32),
+            V((tall, R, 128), F32),
             V((CH, DL), BF),
             V((2, HL * R * T, DL), BF),
             V((HL * R * T, DL), BF),
             V((M, shards * W), F32),
             V((2, NX, NZ, M, 128), F32),
             V((NX, NZ, M, 128), F32),
-            V((2 * max(NX - 1, 1), NZ // 2, M, 128), F32),
+            V((NX, NZ, M, 128), BF),
+            V((NX, NZ, M, 128), BF),
             V((NZ, M, 128), F32),
             V((NZ, M, 128), F32),
             V((G * YP, 128), BF),
             V((G * YP, 128), BF),
             dma((4,)), dma((G,)), dma((G,)), dma((4,)), dma((4,)),
-            dma((2, 2, hop)), dma((2, tall)), dma((2, 2, hop)), dma((2, tall)),
-            dma((2, 2, hop)), dma((2, 2, hop)), dma((2, 2, hop)), dma((2, 2, hop)),
-            dma((tall,)), dma((tall,)), dma((tall,)), dma((tall,)),
-            dma((2, 2, hop)), dma((2, 2, hop)), dma((NZ,)), dma((NZ,)), dma((G,)), dma((G,)),
+            dma((2, 2, hop)), dma((2, tall)), dma((2, tall, 2, hop)), dma((2, tall, tall)),
+            dma((4, 2, hop)), dma((4, 2, hop)), dma((4, 2, hop)), dma((4, 2, hop)),
+            dma((tall, 2)), dma((tall, 2)), dma((tall,)), dma((tall,)),
+            dma((NX,)), dma((NX,)), dma((NZ,)), dma((NZ,)), dma((G,)), dma((G,)),
         ],
         compiler_params=pltpu.CompilerParams(
             collective_id=0, has_side_effects=True, vmem_limit_bytes=60 * 2**20

time: 116 us -> 113 us (0.974); the launches traced: 116 us -> 111 us
  Pallas kernels: 114 us -> 110 us
    pallas_call x1, Pallas kernels: 114 us -> 110 us  [local(): pl.pallas_call(functools.partial(kernel, dims), out_shape=jax.ShapeDtypeS...]
where the time goes in v2:
time: 113 us; the launch traced here: 111 us
  Pallas kernels  110 us (97%)
  local copies, waits for them, and re-layouts  1.31 us (1%)
    pallas_call x1, Pallas kernels, local(): pl.pallas_call(functools.partial(kernel, dims), out_shape=jax.ShapeDtypeS...  110 us

profile of v2, /device:TPU:8, one launch (start us, length us, event | category | flops | bytes accessed | tf_op | source)
XLA Modules:
  0.0 111.5 jit_solution(17562303095662929202)
XLA Ops:
  0.0 0.6 maximum_bitcast_fusion.freq_ref
  0.6 109.5 %shard_map.109 = bf16[48,112]{1,0:T(8,128)(2,1)} custom-call(s32[2,32]{1,0:T(2,128)} %bitcast.15, s32[1,16]{1,0:T(1,128)} %bitcast.16, s32[1,32]{1,0:T(1,128)} %bitcast.17, f32[1,64]{1,0:T(1,128)} %maximum_bitcast_fusion.freq_ref, bf16[48,1536]{1,0:T(8,128)(2,1)} %bitcast.12, bf16[48,576]{1,0:T(8,128)(2,1)} %bitcast.13, bf16[1536,384]{1,0:T(8,128)(2,1)} %wuq_ref.1, ...), custom_call_target="tpu_custom_call" | custom-call | tf_op jit(solution)/shard_map/pallas_call | solution.py:703
  110.2 1.3 %copy.13 = bf16[3,16,112]{2,1,0:T(8,128)(2,1)} copy(bf16[3,16,112]{2,1,0:T(8,128)(2,1)} %bitcast.14) | data formatting | bytes 21504
  (1 shorter events, 0.0 us)

commit v3 on v2

--- a/solution.py
+++ b/solution.py
@@ -46,7 +46,7 @@
     ysend, yrecv, kx, ko, qh, qsend, pq, ck, qall, qp, acc, rsr, st, rss,
     sb, sst, rb, rst, lat, lo, fl, part, po, pr, xs, xr, zs, zr, yos, yor,
     l_s, y_s, y_r, p_s, p_r, a1_s, a1_r, a2_s, a2_r, c_s, c_r, d_s, d_r,
-    e_s, e_r, f_s, f_r, x_s, x_r, z_s, z_r, o_s, o_r,
+    e_s, e_r, f_s, f_r, x_s, x_r, z_s, z_r, o_s, o_r, w_s, w_r,
 ):
     G, NX, NZ, NZL, T, R, HL, PERG, YP, KD, DL, DN, DR, QL, W, SLOTS, QA = dims
     QC = T * 2 * HL
@@ -605,25 +605,31 @@
         flat.append(dot(sel, value).astype(BF))
     flat = jnp.concatenate(flat, 1)
     load_o.wait()
-    part[...] = dot(flat, wov[...])
-    shards = 2 * NX * NZ
-    for s in range(shards):
-        s_pre, rest = divmod(s, 2 * NZL * NX)
-        s_x, rest = divmod(rest, 2 * NZL)
-        s_zl, s_core = divmod(rest, 2)
-        first = s * W // 128
-        off = s * W - first * 128
-        if off + W <= 128:
-            piece = part[:, first * 128 : (first + 1) * 128]
-            if off:
-                piece = pltpu.roll(piece, 128 - off, 1)
-        else:
-            piece = pltpu.roll(part[:, first * 128 : (first + 2) * 128], 256 - off, 1)[:, :128]
-        po[s_core, s_x, s_pre * NZL + s_zl] = piece
-    swap = copy(po.at[1 - core], pr, p_s.at[3], p_r.at[3], partner)
-    swap.start()
-    done.append(swap)
-    swap.wait_recv()
+    group = 2 * NZL * NX
+    swaps = []
+    for g in range(NZ // NZL):
+        span = slice(g * group * W, (g + 1) * group * W)
+        part[:, span] = dot(flat, wov[:, span])
+        for s in range(g * group, (g + 1) * group):
+            s_pre, rest = divmod(s, 2 * NZL * NX)
+            s_x, rest = divmod(rest, 2 * NZL)
+            s_zl, s_core = divmod(rest, 2)
+            first = s * W // 128
+            off = s * W - first * 128
+            if off + W <= 128:
+                piece = part[:, first * 128 : (first + 1) * 128]
+                if off:
+                    piece = pltpu.roll(piece, 128 - off, 1)
+            else:
+                piece = pltpu.roll(part[:, first * 128 : (first + 2) * 128], 256 - off, 1)[:, :128]
+            po[s_core, s_x, s_pre * NZL + s_zl] = piece
+        zz = pl.ds(g * NZL, NZL)
+        c = copy(po.at[1 - core, :, zz], pr.at[:, zz], w_s.at[g], w_r.at[g], partner)
+        c.start()
+        swaps.append(c)
+        done.append(c)
+    for c in swaps:
+        c.wait_recv()
     po[core] = po[core] + pr[...]
     for k in range(1, NX):
         j, dev = x_peer(k)
@@ -753,6 +759,7 @@
             dma((4, 2, hop)), dma((4, 2, hop)), dma((4, 2, hop)), dma((4, 2, hop)),
             dma((tall, 2)), dma((tall, 2)), dma((tall,)), dma((tall,)),
             dma((NX,)), dma((NX,)), dma((NZ,)), dma((NZ,)), dma((G,)), dma((G,)),
+            dma((NZ // NZL,)), dma((NZ // NZL,)),
         ],
         compiler_params=pltpu.CompilerParams(
             collective_id=0, has_side_effects=True, vmem_limit_bytes=60 * 2**20

time: 113 us -> 112 us (level)
  no operation moved by 1% of the time
where the time goes in v3:
time: 112 us; the launch traced here: 111 us
  Pallas kernels  109 us (97%)
  local copies, waits for them, and re-layouts  1.31 us (1%)
    pallas_call x1, Pallas kernels, local(): pl.pallas_call(functools.partial(kernel, dims), out_shape=jax.ShapeDtypeS...  109 us

profile of v3, /device:TPU:8, one launch (start us, length us, event | category | flops | bytes accessed | tf_op | source)
XLA Modules:
  0.0 111.4 jit_solution(1677060595058148528)
XLA Ops:
  0.0 0.6 maximum_bitcast_fusion.freq_ref
  0.6 109.4 %shard_map.109 = bf16[48,112]{1,0:T(8,128)(2,1)} custom-call(s32[2,32]{1,0:T(2,128)} %bitcast.15, s32[1,16]{1,0:T(1,128)} %bitcast.16, s32[1,32]{1,0:T(1,128)} %bitcast.17, f32[1,64]{1,0:T(1,128)} %maximum_bitcast_fusion.freq_ref, bf16[48,1536]{1,0:T(8,128)(2,1)} %bitcast.12, bf16[48,576]{1,0:T(8,128)(2,1)} %bitcast.13, bf16[1536,384]{1,0:T(8,128)(2,1)} %wuq_ref.1, ...), custom_call_target="tpu_custom_call" | custom-call | tf_op jit(solution)/shard_map/pallas_call | solution.py:709
  110.0 1.3 %copy.13 = bf16[3,16,112]{2,1,0:T(8,128)(2,1)} copy(bf16[3,16,112]{2,1,0:T(8,128)(2,1)} %bitcast.14) | data formatting | bytes 21504
  (1 shorter events, 0.0 us)

commit v4 on v3

--- a/solution.py
+++ b/solution.py
@@ -491,6 +491,45 @@
                 for d in range(2):
                     step(q, d, h)
 
+        def line_slot(b, d, h):
+            return b * (n1 - 1) + (0 if d == 0 else hops(n1, b, 0)) + h - 1
+
+        def line_copies(b, d, h, k):
+            _, dev = peer1(1 if d == 0 else n1 - 1)
+            s = line_slot(b, d, h)
+            return (
+                copy(sb.at[k, b], rb.at[s], e_s.at[b, d, h], e_r.at[b, d, h], dev),
+                copy(sst.at[k, b], rst.at[s], f_s.at[b, d, h], f_r.at[b, d, h], dev),
+            )
+
+        def columns(b, g):
+            fill = onehot(part_rows, R, lambda i: b * RB + i // QC)
+            wide = dot(fill, g, precision=lax.Precision.HIGHEST)
+            head = iota((part_rows, 128), 0) % QC
+            return jnp.sum(
+                jnp.where(iota((part_rows, 128), 1) == head, wide, 0.0), axis=1, keepdims=True
+            )
+
+        def line_step(b, d, h):
+            if h > hops(n1, b, d):
+                return
+            ahead = hops(n1, b, d) - h + 1
+            k = ahead if d == 0 else n1 - ahead
+            if h > 1:
+                for c in line_copies(b, d, h - 1, k):
+                    c.wait_recv()
+                s = line_slot(b, d, h - 1)
+                own, came = sst[k, b], rst[s]
+                top = jnp.maximum(own, came)
+                g_own, g_came = jnp.exp(own - top), jnp.exp(came - top)
+                total = g_own + g_came
+                sst[k, b] = top + jnp.log(total)
+                summed = sb[k, b].astype(F32) * columns(b, g_own / total)
+                summed = summed + rb[s].astype(F32) * columns(b, g_came / total)
+                sb[k, b] = summed.astype(BF)
+            for c in line_copies(b, d, h, k):
+                launch(c)
+
         for b in range(2):
             for q in (2 * b, 2 * b + 1):
                 slots = []
@@ -504,46 +543,19 @@
                 if slots:
                     merge(q, i2, slots)
             block = pl.ds(pl.multiple_of(i2 * blk + 2 * b * sub, 16), 2 * sub)
+            stats = jnp.where(iota((R, 128), 0) // RQ == 2 * b, st[2 * b, i2], st[2 * b + 1, i2])
             for k in range(1, n1 + 1):
                 j, dev = peer1(k)
                 sel = onehot(part_rows, 2 * sub, lambda i: i // QC * w + j * QC + i % QC)
-                value = dot(sel.astype(BF), acc[block, :]).astype(BF)
-                if k == n1:
-                    rb[pl.ds(pl.multiple_of(i1 * CH + b * part_rows, 16), part_rows), :] = value
-                    continue
-                sb[k, b * part_rows : (b + 1) * part_rows] = value
-                launch(
-                    copy(
-                        sb.at[k, pl.ds(b * part_rows, part_rows)],
-                        rows(rb, i1 * CH + b * part_rows, part_rows),
-                        e_s.at[k, b],
-                        e_r.at[i1, b],
-                        dev,
-                    )
-                )
-        stats = st[0, i2]
-        for q in range(1, 4):
-            stats = jnp.where(iota((R, 128), 0) // RQ == q, st[q, i2], stats)
-        for k in range(1, n1 + 1):
-            j, dev = peer1(k)
-            sel = onehot(128, 128, lambda i: jnp.where(i // QC == j, i % QC, -1))
-            stat = dot(stats, sel, precision=lax.Precision.HIGHEST)
-            if k == n1:
-                rst[i1] = stat
-                continue
-            sst[k] = stat
-            launch(copy(sst.at[k], rst.at[i1], f_s.at[k], f_r.at[i1], dev))
-        for k in range(1, n1):
-            j, dev = peer1(k)
+                sb[k % n1, b] = dot(sel.astype(BF), acc[block, :]).astype(BF)
+                sel = onehot(128, 128, lambda i: jnp.where(i // QC == j, i % QC, -1))
+                sst[k % n1, b] = dot(stats, sel, precision=lax.Precision.HIGHEST)
+            for d in range(2):
+                line_step(b, d, 1)
+        for h in range(2, n1 // 2 + 1):
             for b in range(2):
-                copy(
-                    sb.at[k, pl.ds(b * part_rows, part_rows)],
-                    rows(rb, j * CH + b * part_rows, part_rows),
-                    e_s.at[k, b],
-                    e_r.at[j, b],
-                    dev,
-                ).wait_recv()
-            copy(sst.at[k], rst.at[j], f_s.at[k], f_r.at[j], dev).wait_recv()
+                for d in range(2):
+                    line_step(b, d, h)
 
         if cc == 0:
             nkv = dot(sels[...], nkv_ref[...]).astype(BF)
@@ -554,23 +566,30 @@
         j = lax.broadcasted_iota(jnp.int32, (CH, M), 1)
         seen = (i // QC == j // T) & (j % T <= i % QC // (2 * HL)) & (j < RT)
         fresh = jnp.where(seen, fresh, NEG)
-        fill = onehot(CH, R, lambda i: i // QC)
-        own_head = lax.broadcasted_iota(jnp.int32, (CH, 128), 0) % QC
-        lane = lax.broadcasted_iota(jnp.int32, (CH, 128), 1)
-        lses = []
-        for s in range(n1):
-            spread_out = dot(fill, rst[s], precision=lax.Precision.HIGHEST)
-            lses.append(
-                jnp.sum(jnp.where(lane == own_head, spread_out, 0.0), axis=1, keepdims=True)
-            )
+        parts = [([sb[0, b] for b in range(2)], [columns(b, sst[0, b]) for b in range(2)])]
+        for d in range(2):
+            values, stats = [], []
+            for b in range(2):
+                last = hops(n1, b, d)
+                if last:
+                    for c in line_copies(b, d, last, 0):
+                        c.wait_recv()
+                    s = line_slot(b, d, last)
+                    values.append(rb[s])
+                    stats.append(columns(b, rst[s]))
+                else:
+                    values.append(jnp.zeros((part_rows, DL), BF))
+                    stats.append(jnp.full((part_rows, 1), NEG, F32))
+            parts.append((values, stats))
+        lses = [jnp.concatenate(stats, 0) for _, stats in parts]
         top = functools.reduce(jnp.maximum, lses, jnp.max(fresh, axis=1, keepdims=True))
         probs = jnp.where(seen, jnp.exp(fresh - top), 0.0)
         total = jnp.sum(probs, axis=1, keepdims=True)
         summed = dot(probs.astype(BF), nkv[:, :DL])
-        for s in range(n1):
-            g = jnp.exp(lses[s] - top)
+        for (values, _), lse in zip(parts, lses):
+            g = jnp.exp(lse - top)
             total = total + g
-            summed = summed + rb[s * CH : (s + 1) * CH, :].astype(F32) * g
+            summed = summed + jnp.concatenate(values, 0).astype(F32) * g
         lat[...] = (summed / total).astype(BF)
         for c in sends:
             c.wait_send()
@@ -738,10 +757,10 @@
             V((rsr_rows, DL), BF),
             V((4, tall, R, 128), F32),
             V((4 * (tall - 1), R, 128), F32),
-            V((tall, CH, DL), BF),
-            V((tall, R, 128), F32),
-            V((tall * CH, DL), BF),
-            V((tall, R, 128), F32),
+            V((tall, 2, CH // 2, DL), BF),
+            V((tall, 2, R, 128), F32),
+            V((2 * (tall - 1), CH // 2, DL), BF),
+            V((2 * (tall - 1), R, 128), F32),
             V((CH, DL), BF),
             V((2, HL * R * T, DL), BF),
             V((HL * R * T, DL), BF),
@@ -757,7 +776,7 @@
             dma((4,)), dma((G,)), dma((G,)), dma((4,)), dma((4,)),
             dma((2, 2, hop)), dma((2, tall)), dma((2, tall, 2, hop)), dma((2, tall, tall)),
             dma((4, 2, hop)), dma((4, 2, hop)), dma((4, 2, hop)), dma((4, 2, hop)),
-            dma((tall, 2)), dma((tall, 2)), dma((tall,)), dma((tall,)),
+            dma((2, 2, hop)), dma((2, 2, hop)), dma((2, 2, hop)), dma((2, 2, hop)),
             dma((NX,)), dma((NX,)), dma((NZ,)), dma((NZ,)), dma((G,)), dma((G,)),
             dma((NZ // NZL,)), dma((NZ // NZL,)),
         ],

time: 112 us -> 111 us (level)
    pallas_call x1, Pallas kernels: 109 us -> 108 us  [local(): pl.pallas_call(functools.partial(kernel, dims), out_shape=jax.ShapeDtypeS...]
where the time goes in v4:
time: 111 us; the launch traced here: 110 us
  Pallas kernels  108 us (97%)
  local copies, waits for them, and re-layouts  1.31 us (1%)
    pallas_call x1, Pallas kernels, local(): pl.pallas_call(functools.partial(kernel, dims), out_shape=jax.ShapeDtypeS...  108 us

profile of v4, /device:TPU:8, one launch (start us, length us, event | category | flops | bytes accessed | tf_op | source)
XLA Modules:
  0.0 109.7 jit_solution(10852181960769622497)
XLA Ops:
  0.0 0.6 maximum_bitcast_fusion.freq_ref
  0.6 107.8 %shard_map.109 = bf16[48,112]{1,0:T(8,128)(2,1)} custom-call(s32[2,32]{1,0:T(2,128)} %bitcast.15, s32[1,16]{1,0:T(1,128)} %bitcast.16, s32[1,32]{1,0:T(1,128)} %bitcast.17, f32[1,64]{1,0:T(1,128)} %maximum_bitcast_fusion.freq_ref, bf16[48,1536]{1,0:T(8,128)(2,1)} %bitcast.12, bf16[48,576]{1,0:T(8,128)(2,1)} %bitcast.13, bf16[1536,384]{1,0:T(8,128)(2,1)} %wuq_ref.1, ...), custom_call_target="tpu_custom_call" | custom-call | tf_op jit(solution)/shard_map/pallas_call | solution.py:728
  108.4 1.3 %copy.13 = bf16[3,16,112]{2,1,0:T(8,128)(2,1)} copy(bf16[3,16,112]{2,1,0:T(8,128)(2,1)} %bitcast.14) | data formatting | bytes 21504
  (1 shorter events, 0.0 us)
